TPU v7x, 256 devices: a whole 4x4x8 slice. The times are simulated.
256 devices in a mesh: group: 4 (over z_hi), dom: 16 (over x, y), pen: 4 (over z_lo, core).
Axes of the slice: x: 4, y: 4, z: 8 (z_hi: 4, z_lo: 2; z = z_hi * 2 + z_lo), core: 2. Of those that a mesh axis runs over, the one named last changes fastest.
Arguments:
- atom_positions: float32 [64, 4, 3, 2048], P(('group', 'dom'), 'pen'), may hold values from 0 to 1
- atom_charges: float32 [64, 4, 2048], P(('group', 'dom'), 'pen'), may hold values from -1.2 to 1.2
- multipole_basis: float32 [64, 4, 4, 2048], P(('group', 'dom'), 'pen'), may hold values from -6 to 6
- spread_cell: int32 [64, 4, 8, 2048], P(('group', 'dom'), 'pen'), may hold values from 0 to 32767
- spread_weight: float32 [64, 4, 8, 2048], P(('group', 'dom'), 'pen'), may hold values from 0 to 0.25
- line_slab: int32 [64, 4, 256, 1], P(('group', 'dom'), 'pen'), may hold values from 0 to 63; in each aligned block of 256 rows (0 to 255, 256 to 511, ..., all dimensions but the last counted through in order) at most 8 rows name the same one
- line_target: int32 [64, 4, 256], P(('group', 'dom'), 'pen'), may hold values from 0 to 63
- neighbour_tiles: int32 [64, 4, 16, 16], P(('group', 'dom'), 'pen'), may hold values from 0 to 143
- live_tiles: int32 [64, 4], P(('group', 'dom'), 'pen'), may hold values from 1 to 16, as said below
- initial_density: float32 [128, 128, 128], P(('group', 'dom'), 'pen'), may hold values from -3 to 3
- susceptibility: float32 [128, 128, 128], P(('group', 'dom'), 'pen'), may hold values from 0.05 to 0.5
- ion_potential: float32 [128, 128, 128], P(('group', 'dom'), 'pen'), may hold values from -6 to 6
Outputs:
- potential: float32 [128, 128, 128], P(('group', 'dom'), 'pen')
- density: float32 [128, 128, 128], P(('group', 'dom'), 'pen')
- mm_potential: float32 [64, 4, 2048], P(('group', 'dom'), 'pen')
Inputs may be any that keep to these rules, and one draw needn't show every extreme that they name: `live_tiles`: every domain has at least one live tile and some domain has all 16 live. `line_slab`: no grid slab is named by more than 8 of the 256 lines of one domain; in some domain one slab is named exactly 8 times.
All inputs are finite; a program needn't handle non-finite values.
Results may differ from a plain program's by a relative error of at most 0.0003.
Values sent between devices are 32-bit elements; how exact they have to be, the bound alone decides.
A program may use at most 64 MiB of HBM per device.

v0:
```python
import math

import jax
import jax.numpy as jnp
from jax import lax
from jax.sharding import PartitionSpec as P

TILE = 128
ITERS = 4


MIX_RATE = 0.3
SCREENING = 0.1
EWALD_BETA = 2.0
SOFTENING = 0.01
BOX_HEIGHT = 4.0


def extended(block, sides, width):
    for axis, dim in sides:
        count = lax.axis_size(axis)
        forward = [(i, i + 1) for i in range(count - 1)]
        backward = [(target, source) for source, target in forward]
        low = lax.ppermute(
            lax.slice_in_dim(block, block.shape[dim] - width, None, axis=dim), axis, forward
        )
        high = lax.ppermute(lax.slice_in_dim(block, 0, width, axis=dim), axis, backward)
        block = jnp.concatenate([low, block, high], axis=dim)
    return block


def dft_tables(length):
    indices = jnp.arange(length, dtype=jnp.int32)
    products = indices[:, None] * indices[None, :] % length
    phase_angle = 2.0 * math.pi / length * products.astype(jnp.float32)
    return (jnp.cos(phase_angle), jnp.sin(phase_angle))


def eigen_values(frequency, length):
    return 2.0 - 2.0 * jnp.cos(2.0 * math.pi / length * frequency.astype(jnp.float32))


def transform_axis(spectrum, axis_number, direction_sign, cosine_table, sine_table):
    einsum_forms = {1: "xbc,xk->kbc", 2: "axc,xk->akc", 3: "abx,xk->abk"}
    pattern = einsum_forms[axis_number]

    def product_along(left, table):
        return jnp.einsum(pattern, left, table, precision=lax.Precision.HIGHEST)

    real_part = spectrum[0]
    imag_part = spectrum[1]
    new_real = product_along(real_part, cosine_table) - direction_sign * product_along(
        imag_part, sine_table
    )
    new_imag = product_along(imag_part, cosine_table) + direction_sign * product_along(
        real_part, sine_table
    )
    return jnp.stack([new_real, new_imag])


def green_factor(freq_x, freq_y, freq_z, length):
    eigen_sum = (
        eigen_values(freq_x, length)[:, None, None]
        + eigen_values(freq_y, length)[None, :, None]
        + eigen_values(freq_z, length)[None, None, :]
    )
    return 1.0 / (SCREENING + eigen_sum)


def solve_field(grid_field, cosine_table, sine_table):
    length = grid_field.shape[2]
    rows_count = lax.axis_size(("group", "dom"))
    pencil_count = lax.axis_size("pen")
    row_index = lax.axis_index(("group", "dom"))
    pencil_index = lax.axis_index("pen")
    row_width = length // rows_count
    pencil_width = length // pencil_count
    first_real = jnp.einsum(
        "abx,xk->abk", grid_field, cosine_table, precision=lax.Precision.HIGHEST
    )
    first_imag = -jnp.einsum("abx,xk->abk", grid_field, sine_table, precision=lax.Precision.HIGHEST)
    spectrum = jnp.stack([first_real, first_imag])

    def forward(axis_number):
        return lambda piece: transform_axis(piece, axis_number, -1.0, cosine_table, sine_table)

    def backward(axis_number):
        return lambda piece: transform_axis(piece, axis_number, 1.0, cosine_table, sine_table)

    spectrum = forward(2)(lax.all_to_all(spectrum, "pen", split_axis=3, concat_axis=2, tiled=True))
    spectrum = forward(1)(
        lax.all_to_all(spectrum, ("group", "dom"), split_axis=2, concat_axis=1, tiled=True)
    )
    freq_x = jnp.arange(length, dtype=jnp.int32)
    freq_y = row_index * row_width + jnp.arange(row_width, dtype=jnp.int32)
    freq_z = pencil_index * pencil_width + jnp.arange(pencil_width, dtype=jnp.int32)
    spectrum = spectrum * green_factor(freq_x, freq_y, freq_z, length)[None]
    spectrum = transform_axis(spectrum, 1, 1.0, cosine_table, sine_table)
    spectrum = backward(2)(
        lax.all_to_all(spectrum, ("group", "dom"), split_axis=1, concat_axis=2, tiled=True)
    )
    spectrum = backward(3)(lax.all_to_all(spectrum, "pen", split_axis=2, concat_axis=3, tiled=True))
    return spectrum[0] / float(length**3)


def tile_block(own_tiles, flat_halo, neighbour_ids, first_tile, tile_count, tiles_per_step):
    chosen = lax.dynamic_slice_in_dim(neighbour_ids, first_tile, tiles_per_step, 0)
    source_tile = chosen // tile_count
    local_tile = chosen % tile_count
    partner = flat_halo[source_tile, :, local_tile]
    offset_x = (source_tile // 3 - 1).astype(jnp.float32)[:, :, None]
    offset_y = (source_tile % 3 - 1).astype(jnp.float32)[:, :, None]
    own_block = lax.dynamic_slice_in_dim(own_tiles, first_tile, tiles_per_step, 1)
    delta_x = own_block[0][:, :, None, None] - (partner[:, :, 0] + offset_x)[:, None]
    delta_y = own_block[1][:, :, None, None] - (partner[:, :, 1] + offset_y)[:, None]
    delta_z = BOX_HEIGHT * (own_block[2][:, :, None, None] - partner[:, :, 2][:, None])
    distance = jnp.sqrt(delta_x * delta_x + delta_y * delta_y + delta_z * delta_z + SOFTENING)
    kernel = jax.scipy.special.erfc(EWALD_BETA * distance) / distance
    return jnp.sum(partner[:, :, 3][:, None] * kernel, axis=(2, 3))


def short_range(own_atoms, beside_all, neighbour_ids, live_count):
    tile_count = own_atoms.shape[1] // TILE
    flat_halo = beside_all.reshape(9, 4, tile_count, TILE)
    own_tiles = own_atoms.reshape(4, tile_count, TILE)
    tiles_per_step = 4
    steps_needed = (live_count + tiles_per_step - 1) // tiles_per_step

    def advance(counter, running):
        first_tile = counter * tiles_per_step
        values = tile_block(
            own_tiles, flat_halo, neighbour_ids, first_tile, tile_count, tiles_per_step
        )
        return lax.dynamic_update_slice_in_dim(running, values, first_tile, 0)

    result = lax.fori_loop(0, steps_needed, advance, jnp.zeros((tile_count, TILE), jnp.float32))
    return result.reshape(-1)


def shards(
    atom_positions,
    atom_charges,
    multipole_basis,
    spread_cell,
    spread_weight,
    line_slab,
    line_target,
    neighbour_tiles,
    live_tiles,
    initial_density,
    susceptibility,
    ion_potential,
):
    positions = atom_positions[0, 0]
    atom_total = positions.shape[1]
    live_count = live_tiles[0, 0]
    live_mask = (jnp.arange(atom_total, dtype=jnp.int32) // TILE < live_count).astype(jnp.float32)
    charge = atom_charges[0, 0] * live_mask
    packed = jnp.concatenate([positions, charge[None, :]], axis=0)[None, None]
    beside_all = extended(packed, ((("group", "dom"), 0), ("pen", 1)), 1)
    cells = spread_cell[0, 0]
    weights = spread_weight[0, 0]
    block_shape = initial_density.shape
    length = block_shape[2]
    cell_total = block_shape[0] * block_shape[1] * block_shape[2]
    lines_dev = cell_total // length
    line_count = line_slab.shape[2]
    charge_lines = jax.ops.segment_sum(
        (weights * charge[None, :]).reshape(-1), cells.reshape(-1), num_segments=line_count * length
    ).reshape(line_count, length)
    slab = line_slab[0, 0, :, 0]
    target = line_target[0, 0]
    dest_id = slab * lines_dev + target
    wanted = jnp.arange(lax.axis_size(("group", "dom")) * lines_dev, dtype=jnp.int32)
    chooser = (dest_id[None, :] == wanted[:, None]).astype(jnp.float32)
    mm_grid = lax.psum_scatter(
        jnp.dot(chooser, charge_lines, precision=lax.Precision.HIGHEST),
        ("group", "dom"),
        scatter_dimension=0,
        tiled=True,
    ).reshape(block_shape)
    short_values = short_range(packed[0, 0], beside_all, neighbour_tiles[0, 0], live_count)
    cosine_table, sine_table = dft_tables(length)
    rho = initial_density
    potential = jnp.zeros_like(rho)
    for iteration in range(ITERS):
        potential = solve_field(rho + mm_grid, cosine_table, sine_table)
        rho = rho - MIX_RATE * (rho + susceptibility * (potential + ion_potential))
    row_index = lax.axis_index(("group", "dom"))
    pencil_index = lax.axis_index("pen")
    global_x = row_index * block_shape[0] + jnp.arange(block_shape[0], dtype=jnp.int32)
    global_y = pencil_index * block_shape[1] + jnp.arange(block_shape[1], dtype=jnp.int32)
    global_z = jnp.arange(length, dtype=jnp.int32)
    coord_x = (1.0 + 2.0 * (global_x.astype(jnp.float32) + 0.5) / length)[:, None, None]
    coord_y = (1.0 + 2.0 * (global_y.astype(jnp.float32) + 0.5) / length)[None, :, None]
    coord_z = (1.0 + 2.0 * (global_z.astype(jnp.float32) + 0.5) / length)[None, None, :]
    local_moments = jnp.stack(
        [
            jnp.sum(rho * coord_x),
            jnp.sum(rho * coord_y),
            jnp.sum(rho * coord_x * coord_y),
            jnp.sum(rho * coord_z),
        ]
    )
    moments = lax.psum(local_moments, ("group", "dom", "pen")) * (
        1.0 / (length * math.sqrt(length))
    )
    potential_lines = potential.reshape(lines_dev, length)
    piece = lax.all_gather(potential_lines, ("group", "dom"), axis=0, tiled=True)
    chooser = (dest_id[:, None] == jnp.arange(piece.shape[0], dtype=jnp.int32)[None, :]).astype(
        jnp.float32
    )
    line_potential = jnp.dot(chooser, piece, precision=lax.Precision.HIGHEST)
    long_range = jnp.sum(weights * jnp.take(line_potential.reshape(-1), cells, axis=0), axis=0)
    far_field = jnp.sum(moments[:, None] * multipole_basis[0, 0], axis=0)
    mm_potential = live_mask * (short_values + long_range + far_field)
    return (potential, rho, mm_potential[None, None])


def solution(mesh):
    placed = (
        P(("group", "dom"), "pen", None, None),
        P(("group", "dom"), "pen", None),
        P(("group", "dom"), "pen", None, None),
        P(("group", "dom"), "pen", None, None),
        P(("group", "dom"), "pen", None, None),
        P(("group", "dom"), "pen", None, None),
        P(("group", "dom"), "pen", None),
        P(("group", "dom"), "pen", None, None),
        P(("group", "dom"), "pen"),
        P(("group", "dom"), "pen", None),
        P(("group", "dom"), "pen", None),
        P(("group", "dom"), "pen", None),
    )
    return jax.shard_map(
        shards,
        mesh=mesh,
        in_specs=placed,
        out_specs=(
            P(("group", "dom"), "pen", None),
            P(("group", "dom"), "pen", None),
            P(("group", "dom"), "pen", None),
        ),
        check_vma=False,
    )
```

profile of v0, /device:TPU:1, one launch (start us, length us, event | category | flops | bytes accessed | tf_op | source)
XLA Modules:
  0.0 1000.4 jit_solution(68633534964549256)
XLA Ops:
  11.7 85.9 %scatter_custom_fusion = f32[32768]{0:T(1024)S(1)} fusion(s32[16384]{0:T(1024)S(1)} %bitcast.694, f32[16384]{0:T(1024)S(1)} %mul.1005, f32[]{:T(128)} %constant.379.clone.1), kind=kCustom, calls=%fused_computation.156 | custom fusion | flops 16384 | bytes 131076 | tf_op jit(solution)/shard_map/scatter-add | solution.py:168
  97.6 3.2 fusion.21
  101.0 338.8 %reduce-scatter.2.cloned.1.call-done = f32[64,128]{1,0:T(8,128)} async-done(((f32[4096,128]{1,0:T(8,128)}), f32[64,128]{1,0:T(8,128)}) %reduce-scatter.2.cloned.1.call-update) | async-done | bytes 32784 | tf_op jit(solution)/shard_map/reduce_scatter | solution.py:176
  439.8 1.2 convolution_bitcast_fusion.4
  441.0 1.2 fusion.46
  443.3 54.7 %all-to-all-start = ((f32[4,1,4096]{2,1,0:T(1,128)}), f32[4,1,4096]{2,1,0:T(1,128)S(1)}, u32[]{:S(2)}, u32[]{:S(2)}) async-start(f32[4,1,4096]{2,1,0:T(1,128)} %reshape.615), calls=%async_computation.1 | async-start | bytes 131072 | tf_op jit(solution)/shard_map/all_to_all | solution.py:90
  498.0 3.2 all-to-all-done
  505.2 0.9 reshape.617
  506.1 4.8 all-to-all-start.1
  511.1 10.9 %all-to-all-done.1 = f32[64,1,256]{2,1,0:T(1,128)S(1)} async-done(((f32[64,1,256]{2,1,0:T(1,128)}), f32[64,1,256]{2,1,0:T(1,128)S(1)}, u32[]{:S(2)}, u32[]{:S(2)}) %all-to-all-start.1) | async-done | bytes 65568 | tf_op jit(solution)/shard_map/all_to_all | solution.py:92
  527.6 15.0 %all_to_all.240 = f32[64,1,256]{2,1,0:T(1,128)S(1)} all-to-all(f32[64,1,256]{2,1,0:T(1,128)S(1)} %reshape.619), channel_id=1, replica_groups=mesh['group'=4,'dom'=16,'pen'=4] {'group','dom'}, dimensions={0} | all-to-all | bytes 131072 | tf_op jit(solution)/shard_map/all_to_all | solution.py:100
  546.4 8.8 all_to_all.241
  559.0 6.9 all_to_all.242
  569.7 15.0 %all_to_all.243 = f32[64,1,256]{2,1,0:T(1,128)S(1)} all-to-all(f32[64,1,256]{2,1,0:T(1,128)S(1)} %reshape.625), channel_id=1, replica_groups=mesh['group'=4,'dom'=16,'pen'=4] {'group','dom'}, dimensions={0} | all-to-all | bytes 131072 | tf_op jit(solution)/shard_map/all_to_all | solution.py:92
  590.4 15.0 %all_to_all.244 = f32[64,1,256]{2,1,0:T(1,128)S(1)} all-to-all(f32[64,1,256]{2,1,0:T(1,128)S(1)} %reshape.627), channel_id=1, replica_groups=mesh['group'=4,'dom'=16,'pen'=4] {'group','dom'}, dimensions={0} | all-to-all | bytes 131072 | tf_op jit(solution)/shard_map/all_to_all | solution.py:100
  609.2 9.2 all_to_all.245
  621.9 0.9 reshape.631
  622.8 4.1 all-to-all-start.8
  627.0 3.2 all-to-all-done.8
  634.6 4.6 all-to-all-start.9
  639.3 2.8 collective-permute-start
  642.1 1.3 collective-permute-start.1
  643.4 6.9 all-to-all-done.9
  656.5 8.2 all-to-all-start.10
  664.7 10.8 %all-to-all-done.10 = f32[64,1,256]{2,1,0:T(1,128)S(1)} async-done(((f32[64,1,256]{2,1,0:T(1,128)}), f32[64,1,256]{2,1,0:T(1,128)S(1)}, u32[]{:S(2)}, u32[]{:S(2)}) %all-to-all-start.10) | async-done | bytes 65568 | tf_op jit(solution)/shard_map/all_to_all | solution.py:100
  680.0 6.4 all-to-all-start.11
  686.4 3.2 all-to-all-done.11
  694.0 4.1 all-to-all-start.12
  698.2 3.2 all-to-all-done.12
  705.9 4.9 all-to-all-start.13
  710.8 11.0 %all-to-all-done.13 = f32[64,1,256]{2,1,0:T(1,128)S(1)} async-done(((f32[64,1,256]{2,1,0:T(1,128)}), f32[64,1,256]{2,1,0:T(1,128)S(1)}, u32[]{:S(2)}, u32[]{:S(2)}) %all-to-all-start.13) | async-done | bytes 65568 | tf_op jit(solution)/shard_map/all_to_all | solution.py:92
  728.0 4.6 all-to-all-start.14
  732.7 3.5 collective-permute-start.2
  736.2 1.9 collective-permute-start.3
  738.2 5.3 all-to-all-done.14
  747.0 0.9 reshape.645
  747.9 6.3 all-to-all-start.15
  754.3 3.2 all-to-all-done.15
  759.4 1.7 multiply_reduce_fusion.3
  761.2 2.5 pad_maximum_fusion.19
  763.7 60.8 %while.13 = (s32[]{:T(128)}, f32[16,128]{1,0:T(8,128)S(1)}, s32[]{:T(128)}, s32[16,16]{1,0:T(8,128)S(1)}, f32[9,4,16,128]{3,1,2,0:T(4,128)S(1)}, /*index=5*/f32[...) while((s32[]{:T(128)}, f32[16,128]{1,0:T(8,128)S(1)}, ...), condition=%wide.region_4.5_spmd, body=%wide.region_2.4_spmd.sunk | while | flops 77614024 | bytes 814547 | solution.py:136
  764.8 14.1 %fusion.662 = f32[4,128]{1,0:T(4,128)S(1)} fusion(f32[4,16,128]{2,1,0:T(8,128)S(1)} %bitcast.668, f32[4,128]{1,0:T(4,128)S(1)} %get-tuple-element.254, f32[4,16,128]{2,1,0:T(8,128)S(1)} %get-tuple-element.259, f32[4,128]{1,0:T(4,128)S(1)} %get-tuple-element.260, f32[4,16,128]{2,1,0:T(8,128)S(1)} %get-tuple-element.261, ...), kind=kLoop, calls=%fused_computation.23.clone.1 | loop fusion | flops 77594112 | bytes 139264 | tf_op jit(solution)/shard_map/while/body/reduce_sum | solution.py:119
  780.0 14.1 %fusion.662 = f32[4,128]{1,0:T(4,128)S(1)} fusion(f32[4,16,128]{2,1,0:T(8,128)S(1)} %bitcast.668, f32[4,128]{1,0:T(4,128)S(1)} %get-tuple-element.254, f32[4,16,128]{2,1,0:T(8,128)S(1)} %get-tuple-element.259, f32[4,128]{1,0:T(4,128)S(1)} %get-tuple-element.260, f32[4,16,128]{2,1,0:T(8,128)S(1)} %get-tuple-element.261, ...), kind=kLoop, calls=%fused_computation.23.clone.1 | loop fusion | flops 77594112 | bytes 139264 | tf_op jit(solution)/shard_map/while/body/reduce_sum | solution.py:119
  795.2 14.1 %fusion.662 = f32[4,128]{1,0:T(4,128)S(1)} fusion(f32[4,16,128]{2,1,0:T(8,128)S(1)} %bitcast.668, f32[4,128]{1,0:T(4,128)S(1)} %get-tuple-element.254, f32[4,16,128]{2,1,0:T(8,128)S(1)} %get-tuple-element.259, f32[4,128]{1,0:T(4,128)S(1)} %get-tuple-element.260, f32[4,16,128]{2,1,0:T(8,128)S(1)} %get-tuple-element.261, ...), kind=kLoop, calls=%fused_computation.23.clone.1 | loop fusion | flops 77594112 | bytes 139264 | tf_op jit(solution)/shard_map/while/body/reduce_sum | solution.py:119
  810.4 14.1 %fusion.662 = f32[4,128]{1,0:T(4,128)S(1)} fusion(f32[4,16,128]{2,1,0:T(8,128)S(1)} %bitcast.668, f32[4,128]{1,0:T(4,128)S(1)} %get-tuple-element.254, f32[4,16,128]{2,1,0:T(8,128)S(1)} %get-tuple-element.259, f32[4,128]{1,0:T(4,128)S(1)} %get-tuple-element.260, f32[4,16,128]{2,1,0:T(8,128)S(1)} %get-tuple-element.261, ...), kind=kLoop, calls=%fused_computation.23.clone.1 | loop fusion | flops 77594112 | bytes 139264 | tf_op jit(solution)/shard_map/while/body/reduce_sum | solution.py:119
  824.5 73.3 %psum.7 = f32[4]{0:T(128)S(1)} all-reduce(f32[4]{0:T(128)S(1)} %pad_maximum_fusion.19), channel_id=1, replica_groups=mesh['group'=4,'dom'=16,'pen'=4] {'group','dom','pen'}, use_global_device_ids=true, to_apply=%region_10.11 | all-reduce | flops 4 | bytes 32 | tf_op jit(solution)/shard_map/psum | solution.py:205
  897.9 3.9 convolution_bitcast_fusion
  901.8 90.5 %gather_fusion.1 = f32[16384]{0:T(1024)S(1)} fusion(f32[32768]{0:T(1024)S(1)} %convolution_bitcast_fusion, s32[16384]{0:T(1024)S(1)} %broadcast_clamp_fusion), kind=kCustom, calls=%fused_computation.1 | custom fusion | bytes 196608 | tf_op jit(solution)/shard_map/jit(_take)/gather | solution.py:214
  (365 shorter events, 78.7 us)
Async XLA Ops:
  7.2 432.6 %reduce-scatter.2.cloned.1.call-start = ((), (), s32[]{:S(2)}) async-start(), calls=%async_computation.17 | async-start | bytes 2129920 | tf_op jit(solution)/shard_map/reduce_scatter | solution.py:176
  97.6 342.2 %copy-start.6 = (f32[2,32,128]{2,1,0:T(8,128)S(1)}, f32[2,32,128]{2,1,0:T(8,128)}, u32[]{:S(2)}) copy-start(f32[2,32,128]{2,1,0:T(8,128)} %param.23) | copy-start | bytes 98308
  443.3 57.9 %all-to-all-start = ((f32[4,1,4096]{2,1,0:T(1,128)}), f32[4,1,4096]{2,1,0:T(1,128)S(1)}, u32[]{:S(2)}, u32[]{:S(2)}) async-start(f32[4,1,4096]{2,1,0:T(1,128)} %reshape.615), calls=%async_computation.1 | async-start | bytes 131072 | tf_op jit(solution)/shard_map/all_to_all | solution.py:90
  506.1 15.8 %all-to-all-start.1 = ((f32[64,1,256]{2,1,0:T(1,128)}), f32[64,1,256]{2,1,0:T(1,128)S(1)}, u32[]{:S(2)}, u32[]{:S(2)}) async-start(f32[64,1,256]{2,1,0:T(1,128)} %reshape.617), calls=%async_computation.2 | async-start | bytes 131072 | tf_op jit(solution)/shard_map/all_to_all | solution.py:92
  544.8 12.4 %copy-start.7 = (f32[2,32,128]{2,1,0:T(8,128)S(1)}, f32[2,32,128]{2,1,0:T(8,128)}, u32[]{:S(2)}) copy-start(f32[2,32,128]{2,1,0:T(8,128)} %param.24) | copy-start | bytes 98308
  544.8 12.4 %copy-start.8 = (f32[2,32,128]{2,1,0:T(8,128)S(1)}, f32[2,32,128]{2,1,0:T(8,128)}, u32[]{:S(2)}) copy-start(f32[2,32,128]{2,1,0:T(8,128)} %param.25) | copy-start | bytes 98308
  544.9 12.7 %copy-start.9 = (f32[64,128]{1,0:T(8,128)S(1)}, f32[64,128]{1,0:T(8,128)}, u32[]{:S(2)}) copy-start(f32[64,128]{1,0:T(8,128)} %reduce-scatter.2.cloned.1.call-done) | copy-start | bytes 98308
  609.1 17.8 %copy-start.3 = (f32[1,1,2048]{2,1,0:T(1,128)S(1)}, f32[1,1,2048]{2,1,0:T(1,128)}, u32[]{:S(2)}) copy-start(f32[1,1,2048]{2,1,0:T(1,128)} %param.15) | copy-start | bytes 24580
  609.1 17.8 %copy-start.2 = (f32[1,1,3,2048]{3,1,2,0:T(1,128)S(1)}, f32[1,1,3,2048]{3,1,2,0:T(1,128)}, u32[]{:S(2)}) copy-start(f32[1,1,3,2048]{3,1,2,0:T(1,128)} %param.14) | copy-start | bytes 73732
  622.8 7.4 all-to-all-start.8
  634.6 15.6 %all-to-all-start.9 = ((f32[64,1,256]{2,1,0:T(1,128)}), f32[64,1,256]{2,1,0:T(1,128)S(1)}, u32[]{:S(2)}, u32[]{:S(2)}) async-start(f32[64,1,256]{2,1,0:T(1,128)} %reshape.633), calls=%async_computation.10 | async-start | bytes 131072 | tf_op jit(solution)/shard_map/all_to_all | solution.py:92
  639.3 93.4 %collective-permute-start = (f32[1,1,4,2048]{3,2,1,0:T(4,128)S(1)}, f32[1,1,4,2048]{3,2,1,0:T(4,128)S(1)}, u32[]{:S(2)}, u32[]{:S(2)}) collective-permute-start(f32[1,1,4,2048]{3,2,1,0:T(4,128)S(1)} %maximum_bitcast_fusion), channel_id=1, source_target_pairs={{0,4},{4,8},{8,12},{12,16},{16,20},{20,24},{24,28},{28,32},{32,36}... | collective-permute-start | bytes 98312 | tf_op jit(solution)/shard_map/ppermute | solution.py:24
  642.1 90.6 %collective-permute-start.1 = (f32[1,1,4,2048]{3,2,1,0:T(4,128)S(1)}, f32[1,1,4,2048]{3,2,1,0:T(4,128)S(1)}, u32[]{:S(2)}, u32[]{:S(2)}) collective-permute-start(f32[1,1,4,2048]{3,2,1,0:T(4,128)S(1)} %maximum_bitcast_fusion), channel_id=1, source_target_pairs={{4,0},{8,4},{12,8},{16,12},{20,16},{24,20},{28,24},{32,28},{36,32}... | collective-permute-start | bytes 98312 | tf_op jit(solution)/shard_map/ppermute | solution.py:27
  651.5 13.2 %copy-start = (s32[1,1,8,2048]{3,2,1,0:T(8,128)S(1)}, s32[1,1,8,2048]{3,2,1,0:T(8,128)}, u32[]{:S(2)}) copy-start(s32[1,1,8,2048]{3,2,1,0:T(8,128)} %param.17) | copy-start | bytes 196612
  656.5 19.1 %all-to-all-start.10 = ((f32[64,1,256]{2,1,0:T(1,128)}), f32[64,1,256]{2,1,0:T(1,128)S(1)}, u32[]{:S(2)}, u32[]{:S(2)}) async-start(f32[64,1,256]{2,1,0:T(1,128)} %reshape.635), calls=%async_computation.11 | async-start | bytes 131072 | tf_op jit(solution)/shard_map/all_to_all | solution.py:100
  680.0 9.6 all-to-all-start.11
  694.0 7.4 all-to-all-start.12
  705.9 15.9 %all-to-all-start.13 = ((f32[64,1,256]{2,1,0:T(1,128)}), f32[64,1,256]{2,1,0:T(1,128)S(1)}, u32[]{:S(2)}, u32[]{:S(2)}) async-start(f32[64,1,256]{2,1,0:T(1,128)} %reshape.641), calls=%async_computation.14 | async-start | bytes 131072 | tf_op jit(solution)/shard_map/all_to_all | solution.py:92
  728.0 15.5 %all-to-all-start.14 = ((f32[64,1,256]{2,1,0:T(1,128)}), f32[64,1,256]{2,1,0:T(1,128)S(1)}, u32[]{:S(2)}, u32[]{:S(2)}) async-start(f32[64,1,256]{2,1,0:T(1,128)} %reshape.643), calls=%async_computation.15 | async-start | bytes 131072 | tf_op jit(solution)/shard_map/all_to_all | solution.py:100
  732.7 21.5 %collective-permute-start.2 = (f32[3,1,4,2048]{3,2,1,0:T(4,128)S(1)}, f32[3,1,4,2048]{3,2,1,0:T(4,128)S(1)}, u32[]{:S(2)}, u32[]{:S(2)}) collective-permute-start(f32[3,1,4,2048]{3,2,1,0:T(4,128)S(1)} %pad_maximum_fusion.1), channel_id=1, source_target_pairs={{0,1},{1,2},{2,3},{4,5},{5,6},{6,7},{8,9},{9,10},{10,11},{12,13},{... | collective-permute-start | bytes 294920 | tf_op jit(solution)/shard_map/ppermute | solution.py:24
  736.2 18.0 %collective-permute-start.3 = (f32[3,1,4,2048]{3,2,1,0:T(4,128)S(1)}, f32[3,1,4,2048]{3,2,1,0:T(4,128)S(1)}, u32[]{:S(2)}, u32[]{:S(2)}) collective-permute-start(f32[3,1,4,2048]{3,2,1,0:T(4,128)S(1)} %pad_maximum_fusion.1), channel_id=1, source_target_pairs={{1,0},{2,1},{3,2},{5,4},{6,5},{7,6},{9,8},{10,9},{11,10},{13,12},{... | collective-permute-start | bytes 294920 | tf_op jit(solution)/shard_map/ppermute | solution.py:27
  746.8 16.9 %copy-start.4 = (s32[1,1,16,16]{3,2,1,0:T(8,128)S(1)}, s32[1,1,16,16]{3,2,1,0:T(8,128)}, u32[]{:S(2)}) copy-start(s32[1,1,16,16]{3,2,1,0:T(8,128)} %param.21) | copy-start | bytes 3076
  747.9 9.5 all-to-all-start.15
  754.2 143.7 %all-gather.2.cloned.1.call-start = ((), (), s32[]{:S(2)}) async-start(), calls=%async_computation.18 | async-start | bytes 2129920 | tf_op jit(solution)/shard_map/all_gather | solution.py:209
  763.7 134.1 %copy-start.5 = (f32[1,1,4,2048]{3,2,1,0:T(4,128)S(1)}, f32[1,1,4,2048]{3,2,1,0:T(4,128)}, u32[]{:S(2)}) copy-start(f32[1,1,4,2048]{3,2,1,0:T(4,128)} %param.16) | copy-start | bytes 98308
  901.8 90.6 %copy-start.1 = (f32[1,1,8,2048]{3,2,1,0:T(8,128)S(1)}, f32[1,1,8,2048]{3,2,1,0:T(8,128)}, u32[]{:S(2)}) copy-start(f32[1,1,8,2048]{3,2,1,0:T(8,128)} %param.18) | copy-start | bytes 196612
Sparse Core Ops, SparseCore 0:
  100.9 338.7 reduce-scatter.1
  761.3 70.1 all-gather.1
where the time goes:
time: 1010 us; the launch traced here: 1000 us
  waiting for transfers between devices  400 us (40%)
  other arithmetic  162 us (16%)
  blocking collectives  143 us (14%)
  local copies, waits for them, and re-layouts  121 us (12%)
  starting transfers between devices  112 us (11%)
  matrix products  45.3 us (4%)
  between operations  17.4 us (2%)
    reduce_scatter x1, waiting for transfers between devices, shards(): lax.psum_scatter(jnp.dot(chooser, charge_lines, precision=lax.Precision.H...  339 us
    gather x2, local copies, waits for them, and re-layouts, shards(): jnp.take(line_potential.reshape(-1), cells, axis=0)  90.6 us
    scatter-add x1, other arithmetic, shards(): jax.ops.segment_sum((weights * charge[None, :]).reshape(-1), cells.reshap...  85.9 us
    psum x1, blocking collectives, shards(): lax.psum(local_moments, ('group', 'dom', 'pen'))  73.3 us
    all_to_all x3, starting transfers between devices, solve_field(): lax.all_to_all(spectrum, 'pen', split_axis=3, concat_axis=2, tiled=True)  62.9 us
    reduce_sum x4, other arithmetic, tile_block(): return jnp.sum(partner[:, :, 3][:, None] * kernel, axis=(2, 3))  56.3 us
    all_to_all x2, blocking collectives, solve_field(): lax.all_to_all(spectrum, ('group', 'dom'), split_axis=1, concat_axis=2, t...  29.9 us
    all_to_all x3, waiting for transfers between devices, solve_field(): lax.all_to_all(spectrum, ('group', 'dom'), split_axis=2, concat_axis=1, t...  28.8 us
  transfers between devices with their start and end apart: 16, of which 11 were waited for; matrix products, arithmetic and copies ran while one was open for 9% of the time, Pallas kernels for 0%

commit v1 on v0

v1 whole, which is shorter than its diff:
```python
import functools
import math

import jax
import jax.numpy as jnp
import ml_dtypes
import numpy as np
from jax import lax
from jax.experimental import pallas as pl
from jax.experimental.pallas import tpu as pltpu
from jax.sharding import PartitionSpec as P

MESH = pl.DeviceIdType.MESH
F32 = jnp.float32
BF16 = jnp.bfloat16
G = 128
TILE = 128
TILES = 16
NBR = 16
ITERS = 4
ROWS = 64
PEN = 4
CAP = 8
NLINES = 256
MIX_RATE = 0.3
SCREENING = 0.1
BOX_HEIGHT = 4.0
SOFTENING = 0.01
ERF_SHIFT = 1.35
ERF_POLY = (
    8.048848463632075e-05,
    0.279831566396696,
    0.40782855654035,
    0.3006583844815809,
    1.260144403309312,
    -1.158323294058104,
    2.9062706842895354,
    -1.262709002135607,
)
VMEM_LIMIT = 48 * 1024 * 1024


def halves(table):
    high = table.astype(ml_dtypes.bfloat16)
    low = (table - high.astype(np.float64)).astype(ml_dtypes.bfloat16)
    return [high, low]


def tables():
    k = np.arange(G)
    angle = 2.0 * np.pi * (np.outer(k, k) % G) / G
    cas = (np.cos(angle) + np.sin(angle)) / np.sqrt(G)
    order = np.concatenate([np.arange(32) + 32 * (2 * z + c) for c in range(2) for z in range(2)])
    split_x = np.concatenate([np.arange(ROWS) * 2, np.arange(ROWS) * 2 + 1])
    square = halves(cas) + halves(cas[:, order]) + halves(cas[:, split_x]) + halves(cas[split_x, :])
    wide = np.zeros((2, G, 2, 2, ROWS))
    for x in range(2):
        for h in range(2):
            wide[x, :, h, x, :] = cas[:, h * ROWS : (h + 1) * ROWS]
    wide = wide.reshape(2 * G, 2 * G)
    big = halves(wide) + halves(wide.T)
    lam = 2.0 - 2.0 * np.cos(2.0 * np.pi * k / G)
    lam_rows = np.repeat(lam[:, None], G, axis=1)
    lam_lanes = np.zeros((8, G))
    for h in range(2):
        lam_lanes[h] = np.tile(lam[h * ROWS : (h + 1) * ROWS], 2)
    flat = np.concatenate([lam_rows, lam_lanes]).astype(np.float32)
    return np.stack(square), np.stack(big), flat


def split(x):
    high = x.astype(BF16)
    return high, (x - high.astype(F32)).astype(BF16)


def dot(a, b):
    return jnp.dot(a, b, preferred_element_type=F32)


def dot_nt(a, b):
    return lax.dot_general(a, b, (((1,), (1,)), ((), ())), preferred_element_type=F32)


def dot_tn(a, b):
    return lax.dot_general(a, b, (((0,), (0,)), ((), ())), preferred_element_type=F32)


def left_const(high, low, x):
    x_high, x_low = split(x)
    return dot(high, x_high) + (dot(high, x_low) + dot(low, x_high))


def right_const(x, high, low):
    x_high, x_low = split(x)
    return dot(x_high, high) + (dot(x_low, high) + dot(x_high, low))


def iota(shape, dim):
    return lax.broadcasted_iota(jnp.int32, shape, dim)


CHUNK = 512


def spread_kernel(
    live_ref, cell_ref, weight_ref, charge_row_ref, positions_ref, charge_ref,
    slab_col_ref, slab_row_ref, target_row_ref, send_ref, packed_ref, slot_ref,
):
    live = live_ref[0, 0]
    tile_of = iota((TILES, TILE), 0)
    for axis in range(3):
        packed_ref[axis * TILES : (axis + 1) * TILES, :] = positions_ref[axis]
    packed_ref[3 * TILES : 4 * TILES, :] = jnp.where(tile_of < live, charge_ref[...], 0.0)
    packed_ref[4 * TILES : 4 * TILES + 8, :] = jnp.zeros((8, TILE), F32) + live.astype(F32)

    slab_row = slab_row_ref[...]
    same = (slab_col_ref[...] == slab_row) & (iota((NLINES, NLINES), 0) < iota((NLINES, NLINES), 1))
    rank = jnp.sum(same.astype(F32), axis=0, keepdims=True).astype(jnp.int32)
    slot = slab_row * CAP + rank
    slot_ref[...] = slot
    pick = (iota((ROWS * CAP, NLINES), 0) == slot).astype(F32).astype(BF16)
    owner = jnp.where(iota((ROWS, NLINES), 0) == slab_row, target_row_ref[...].astype(F32), 0.0)
    place = (iota((TILE, NLINES), 0) == rank).astype(F32)
    targets = dot_nt(owner.astype(BF16), place.astype(BF16))

    line_iota = iota((NLINES, CHUNK), 0)
    cell_iota = iota((G, CHUNK), 0)

    def step(chunk, total):
        where = pl.ds(pl.multiple_of(chunk * CHUNK, CHUNK), CHUNK)
        atom = chunk * CHUNK + iota((1, CHUNK), 1)
        charge = jnp.where(atom // TILE < live, charge_row_ref[:, where], 0.0)
        for corner in range(8):
            cell = cell_ref[corner : corner + 1, where]
            high, low = split(weight_ref[corner : corner + 1, where] * charge)
            hit = line_iota == cell // G
            lines = jnp.concatenate(
                [
                    jnp.where(hit, high.astype(F32), 0.0).astype(BF16),
                    jnp.where(hit, low.astype(F32), 0.0).astype(BF16),
                ],
                axis=0,
            )
            spots = (cell_iota == cell % G).astype(F32).astype(BF16)
            total = total + dot_nt(lines, spots)
        return total

    total = lax.fori_loop(
        0, TILES * TILE // CHUNK, step, jnp.zeros((2 * NLINES, G), F32)
    )
    lines_high, lines_low = split(total[:NLINES] + total[NLINES:])
    send_ref[:, :CAP, :] = (dot(pick, lines_high) + dot(pick, lines_low)).reshape(ROWS, CAP, G)
    send_ref[:, CAP, :] = targets
    send_ref[:, CAP + 1 :, :] = jnp.zeros((ROWS, 16 - CAP - 1, G), F32)


def field_kernel(
    send_ref, packed_ref, rho_ref, sus_ref, ion_ref, square_ref, big_ref, flat_ref,
    pot_out, rho_out, halo_ref, back_ref,
    line_buf, mm, rho, sus, ion, fwd_send, fwd_recv, ret_send, ret_recv, green, line_send, last_pot,
    line_sems, pen_sems, mm_sems, halo_send_sems, halo_recv_sems, fwd_sems, ret_sems, core_sems, back_sems,
):
    group, dom, pen = lax.axis_index("group"), lax.axis_index("dom"), lax.axis_index("pen")
    me = group * 16 + dom
    core, z_lo = lax.rem(pen, 2), pen // 2
    other_chip = lax.rem(pen + 2, PEN)
    sibling = z_lo * 2 + (1 - core)

    def device(row, column):
        return (row // 16, lax.rem(row, 16), column)

    def remote(src, dst, send_sem, recv_sem, row, column):
        return pltpu.make_async_remote_copy(
            src_ref=src, dst_ref=dst, send_sem=send_sem, recv_sem=recv_sem,
            device_id=device(row, column), device_id_type=MESH,
        )

    barrier = pltpu.get_barrier_semaphore()

    def greet(k, carry):
        row = lax.rem(me + k, ROWS)
        pl.semaphore_signal(barrier, inc=1, device_id=device(row, pen), device_id_type=MESH)
        pl.semaphore_signal(barrier, inc=1, device_id=device(row, other_chip), device_id_type=MESH)
        return carry

    lax.fori_loop(1, ROWS, greet, 0)
    for k in (1, 2, 3):
        pl.semaphore_signal(
            barrier, inc=1, device_id=device(me, lax.rem(pen + k, PEN)), device_id_type=MESH
        )
    for dx in (1, ROWS - 1):
        for dy in (1, PEN - 1):
            pl.semaphore_signal(
                barrier, inc=1, device_id=device(lax.rem(me + dx, ROWS), lax.rem(pen + dy, PEN)),
                device_id_type=MESH,
            )
    pl.semaphore_wait(barrier, 2 * (ROWS - 1) + 3 + 4)

    def send_lines(k, carry):
        row = lax.rem(me + k, ROWS)
        remote(
            send_ref.at[row, pl.ds(0, CAP + 1)], line_buf.at[me, pl.ds(0, CAP + 1)],
            line_sems.at[0], line_sems.at[1], row, pen,
        ).start()
        return carry

    lax.fori_loop(1, ROWS, send_lines, 0)
    line_buf[me] = send_ref[me]

    columns = pl.ds(pl.multiple_of(pen * 32, 32), 32)
    slabs = ((rho_ref, rho), (sus_ref, sus), (ion_ref, ion))

    def slab_copy(index, k):
        source, whole = slabs[index]
        return remote(
            source, whole.at[:, columns, :],
            pen_sems.at[0, index, k - 1], pen_sems.at[1, index, k - 1],
            me, lax.rem(pen + k, PEN),
        )

    for index in range(3):
        for k in (1, 2, 3):
            slab_copy(index, k).start()

    neighbours = [(dx, dy) for dx in (-1, 0, 1) for dy in (-1, 0, 1) if (dx, dy) != (0, 0)]

    def halo_copy(dx, dy):
        number = (1 - dx) * 3 + 1 - dy
        return remote(
            packed_ref, halo_ref.at[number], halo_send_sems.at[number], halo_recv_sems.at[number],
            lax.rem(me + dx + ROWS, ROWS), lax.rem(pen + dy + PEN, PEN),
        )

    for dx, dy in neighbours:
        halo_copy(dx, dy).start()

    halo_ref[4] = packed_ref[...]
    for source, whole in slabs:
        whole[:, columns, :] = source[...]

    lane = iota((G, G), 1)
    half = me // 32
    y_row = pen * 32 + lax.rem(me, 32)
    lam_yz = flat_ref[pl.ds(y_row, 1), :] + flat_ref[pl.ds(G + half, 1), :]
    green[...] = 1.0 / (SCREENING + (flat_ref[0:G, :] + lam_yz))

    def whole_line_copy(ref, sems):
        return pltpu.make_async_remote_copy(
            src_ref=ref.at[pl.ds(0, ROWS - 1), pl.ds(0, CAP + 1)],
            dst_ref=ref.at[pl.ds(0, ROWS - 1), pl.ds(0, CAP + 1)],
            send_sem=sems.at[0], recv_sem=sems.at[1],
            device_id=device(lax.rem(me + 1, ROWS), pen), device_id_type=MESH,
        )

    whole_line_copy(line_buf, line_sems).wait_recv()
    source_of = iota((ROWS * CAP, ROWS), 0) // CAP == iota((ROWS * CAP, ROWS), 1)
    spread_targets = dot(source_of.astype(F32).astype(BF16), line_buf[:, CAP, :].astype(BF16))
    own_lane = iota((ROWS * CAP, G), 1) == lax.rem(iota((ROWS * CAP, G), 0), CAP)
    target = jnp.sum(jnp.where(own_lane, spread_targets, 0.0), axis=1, keepdims=True)
    landing = (target == iota((ROWS * CAP, ROWS), 1).astype(F32)).astype(F32)
    landing_t = landing.T.astype(BF16)
    landing = landing.astype(BF16)
    lines_high, lines_low = split(line_buf[:, :CAP, :].reshape(ROWS * CAP, G))
    own_mm = dot(landing_t, lines_high) + dot(landing_t, lines_low)
    for x in range(2):
        mm[x, columns, :] = own_mm[x * 32 : (x + 1) * 32]

    def mm_copy(k):
        return remote(
            mm.at[:, columns, :], mm.at[:, columns, :], mm_sems.at[0, k - 1], mm_sems.at[1, k - 1],
            me, lax.rem(pen + k, PEN),
        )

    for k in (1, 2, 3):
        mm_copy(k).start()
    for index in range(3):
        for k in (1, 2, 3):
            slab_copy(index, k).wait_recv()
    for k in (1, 2, 3):
        mm_copy(k).wait_recv()

    low_lanes = iota((ROWS, G), 1) < ROWS
    chunk_rows = pl.ds(pl.multiple_of(pen * 32, 32), 32)

    def fwd_all():
        return pltpu.make_async_remote_copy(
            src_ref=fwd_send.at[pl.ds(0, ROWS - 1)], dst_ref=fwd_recv.at[pl.ds(0, ROWS - 1)],
            send_sem=fwd_sems.at[0], recv_sem=fwd_sems.at[1],
            device_id=device(lax.rem(me + 1, ROWS), pen), device_id_type=MESH,
        )

    def ret_copy(slot, row, column):
        return remote(
            ret_send.at[pl.ds(row, 1)],
            ret_recv.at[slot, half, core, z_lo, pl.ds(lax.rem(me, 32), 1)],
            ret_sems.at[0], ret_sems.at[1 + slot], row, column,
        )

    def ret_all(slot):
        most = ret_send.at[pl.ds(0, 2 * ROWS - 1)]
        return pltpu.make_async_remote_copy(
            src_ref=most, dst_ref=most,
            send_sem=ret_sems.at[0], recv_sem=ret_sems.at[1 + slot],
            device_id=device(lax.rem(me + 1, ROWS), pen), device_id_type=MESH,
        )

    def core_copy(slot, h):
        return remote(
            ret_recv.at[slot, h, core], ret_recv.at[slot, h, core],
            core_sems.at[0, slot, h], core_sems.at[1, slot, h], me, sibling,
        )

    for iteration in range(ITERS):
        slot = iteration % 2
        source = jnp.concatenate([rho[0] + mm[0], rho[1] + mm[1]], axis=1)
        spectrum = left_const(square_ref[0, chunk_rows, :], square_ref[1, chunk_rows, :], source)
        spectrum = right_const(spectrum, big_ref[0], big_ref[1])
        if iteration > 0:
            fwd_all().wait_send()
        fwd_send[0:32, :] = spectrum[:, :G]
        fwd_send[32:64, :] = spectrum[:, G:]

        def send_fwd(k, carry):
            row = lax.rem(me + k, ROWS)
            remote(
                fwd_send.at[pl.ds(row, 1)], fwd_recv.at[pl.ds(me, 1)],
                fwd_sems.at[0], fwd_sems.at[1], row, pen,
            ).start()
            return carry

        lax.fori_loop(1, ROWS, send_fwd, 0)
        fwd_recv[pl.ds(me, 1), :] = fwd_send[pl.ds(me, 1), :]
        fwd_all().wait_recv()
        received = fwd_recv[...]
        both = jnp.concatenate([received, pltpu.roll(received, ROWS, 1)], axis=0)
        modes = left_const(square_ref[4], square_ref[5], both) * green[...]
        solved = left_const(square_ref[6], square_ref[7], modes)
        if iteration > 0:
            ret_all(1 - slot).wait_send()
        ret_send[:ROWS, :] = jnp.where(low_lanes, solved[:ROWS], pltpu.roll(solved[ROWS:], ROWS, 1))

        def send_ret(k, carry):
            row = lax.rem(me + k, ROWS)
            ret_copy(slot, row, pen).start()
            ret_copy(slot, row, other_chip).start()
            return carry

        lax.fori_loop(1, ROWS, send_ret, 0)
        ret_copy(slot, me, other_chip).start()
        ret_recv[slot, half, core, z_lo, pl.ds(lax.rem(me, 32), 1)] = ret_send[pl.ds(me, 1), :]
        ret_all(slot).wait_recv()
        for h in range(2):
            core_copy(slot, h).start()
        for h in range(2):
            core_copy(slot, h).wait_recv()
        lines = jnp.concatenate([ret_recv[slot, h].reshape(G, G) for h in range(2)], axis=1)
        lines = right_const(lines, big_ref[2], big_ref[3])
        potential = left_const(square_ref[2], square_ref[3], lines)
        for x in range(2):
            own = potential[:, x * G : (x + 1) * G]
            if iteration == ITERS - 1:
                last_pot[x] = own
            rho[x] = rho[x] - MIX_RATE * (rho[x] + sus[x] * (own + ion[x]))
        for h in range(2):
            core_copy(slot, h).wait_send()

    row_u = 1.0 + 2.0 * (iota((G, G), 0).astype(F32) + 0.5) / G
    lane_u = 1.0 + 2.0 * (lane.astype(F32) + 0.5) / G
    x_u = [1.0 + 2.0 * ((2 * me + x).astype(F32) + 0.5) / G for x in range(2)]
    weighted = rho[0] * x_u[0] + rho[1] * x_u[1]
    plain = rho[0] + rho[1]
    sums = [weighted, plain * row_u, weighted * row_u, plain * lane_u]
    own_moments = jnp.zeros((1, G), F32)
    for index, term in enumerate(sums):
        value = jnp.sum(jnp.sum(term, axis=0, keepdims=True), axis=1, keepdims=True)
        own_moments = jnp.where(iota((1, G), 1) == index, value, own_moments)
    own_pot = jnp.concatenate([last_pot[x, columns, :] for x in range(2)], axis=0)
    pot_high, pot_low = split(own_pot)
    line_send[:, :CAP, :] = (dot(landing, pot_high) + dot(landing, pot_low)).reshape(ROWS, CAP, G)
    line_send[:, CAP, :] = jnp.broadcast_to(own_moments, (ROWS, G))

    def send_back(k, carry):
        row = lax.rem(me + k, ROWS)
        remote(
            line_send.at[row, pl.ds(0, CAP + 1)], back_ref.at[me, pl.ds(0, CAP + 1)],
            back_sems.at[0], back_sems.at[1], row, pen,
        ).start()
        return carry

    lax.fori_loop(1, ROWS, send_back, 0)
    back_ref[me, 0 : CAP + 1, :] = line_send[me, 0 : CAP + 1, :]
    for x in range(2):
        pot_out[x] = last_pot[x, columns, :]
        rho_out[x] = rho[x, columns, :]

    last = (ITERS - 1) % 2
    for dx, dy in neighbours:
        halo_copy(dx, dy).wait()
    for dx, dy in neighbours:
        outside = (me + dx < 0) | (me + dx >= ROWS) | (pen + dy < 0) | (pen + dy >= PEN)

        @pl.when(outside)
        def _():
            halo_ref[(dx + 1) * 3 + dy + 1] = jnp.zeros_like(packed_ref)

    whole_line_copy(line_buf, line_sems).wait_send()
    for k in (1, 2, 3):
        for index in range(3):
            slab_copy(index, k).wait_send()
        mm_copy(k).wait_send()
    fwd_all().wait_send()
    ret_all(last).wait_send()
    whole_line_copy(line_send, back_sems).wait()


def pair_values(own, partner, rows):
    x, y, z = own
    dx = x - partner[0]
    dy = y - partner[1]
    dz = z - partner[2]
    s = dx * dx + dy * dy + dz * dz + SOFTENING
    u = lax.rsqrt(s)
    t = 1.0 / (s * u + ERF_SHIFT)
    poly = jnp.full_like(t, ERF_POLY[-1])
    for coefficient in ERF_POLY[-2::-1]:
        poly = poly * t + coefficient
    return (partner[3] * u) * (poly * jnp.exp(-4.0 * s))


def atom_kernel(
    live_ref, nbr_ref, halo_ref, back_ref, slot_ref, cell_ref, weight_ref, basis_ref, out_ref,
    columns, acc, short,
):
    live = live_ref[0, 0]
    for axis in range(3):
        columns[axis] = halo_ref[4, axis * TILES : (axis + 1) * TILES, :].T * (
            BOX_HEIGHT if axis == 2 else 1.0
        )
    live_of = [jnp.max(halo_ref[d, 4 * TILES : 4 * TILES + 1, :]) for d in range(9)]
    tile_lane = iota((TILE, TILES), 1)

    def own_tile(t, carry):
        own = [
            jnp.sum(jnp.where(tile_lane == t, columns[axis], 0.0), axis=1, keepdims=True)
            for axis in range(3)
        ]
        own = [jnp.broadcast_to(c, (TILE, TILE)) for c in own]
        acc[...] = jnp.zeros_like(acc)

        def partner_tile(n, carry):
            chosen = nbr_ref[t, n]
            d = chosen // TILES
            tile = lax.rem(chosen, TILES)
            there = live_of[0]
            for index in range(1, 9):
                there = jnp.where(d == index, live_of[index], there)

            @pl.when(tile.astype(F32) < there)
            def _():
                row = [halo_ref[d, pl.ds(axis * TILES + tile, 1), :] for axis in range(4)]
                row[0] = row[0] + (d // 3 - 1).astype(F32)
                row[1] = row[1] + (lax.rem(d, 3) - 1).astype(F32)
                row[2] = row[2] * BOX_HEIGHT
                for part in range(4):
                    rows = slice(part * 32, part * 32 + 32)
                    acc[rows, :] += pair_values([c[rows, :] for c in own], row, rows)

            return carry

        lax.fori_loop(0, NBR, partner_tile, 0)
        short[:, pl.ds(pl.multiple_of(t * TILE, TILE), TILE)] = jnp.sum(
            acc[...].T, axis=0, keepdims=True
        )
        return carry

    lax.fori_loop(0, live, own_tile, 0)

    slot = slot_ref[...]
    pick = (iota((ROWS * CAP, NLINES), 0) == slot).astype(F32).astype(BF16)
    back_high, back_low = split(back_ref[:, :CAP, :].reshape(ROWS * CAP, G))
    values = dot_tn(jnp.concatenate([back_high, back_low], axis=1), pick)
    values_high, values_low = split(values[:G] + values[G:])
    values = jnp.concatenate([values_high, values_low], axis=0)
    moments = jnp.sum(back_ref[:, CAP, :], axis=0, keepdims=True) * (1.0 / (G * math.sqrt(G)))
    moment = [
        jnp.sum(jnp.where(iota((1, G), 1) == m, moments, 0.0), axis=1, keepdims=True)
        for m in range(4)
    ]
    line_iota = iota((NLINES, CHUNK), 0)
    cell_iota = iota((G, CHUNK), 0)

    def step(chunk, carry):
        where = pl.ds(pl.multiple_of(chunk * CHUNK, CHUNK), CHUNK)
        total = jnp.zeros((1, CHUNK), F32)
        for corner in range(8):
            cell = cell_ref[corner : corner + 1, where]
            lines = (line_iota == cell // G).astype(F32).astype(BF16)
            found = dot(values, lines)
            found = jnp.where(cell_iota == cell % G, found[:G] + found[G:], 0.0)
            total = total + weight_ref[corner : corner + 1, where] * jnp.sum(
                found, axis=0, keepdims=True
            )
        for m in range(4):
            total = total + moment[m] * basis_ref[m : m + 1, where]
        atom = chunk * CHUNK + iota((1, CHUNK), 1)
        out_ref[:, where] = jnp.where(atom // TILE < live, total + short[:, where], 0.0)
        return carry

    lax.fori_loop(0, TILES * TILE // CHUNK, step, 0)


def shards(
    atom_positions, atom_charges, multipole_basis, spread_cell, spread_weight, line_slab,
    line_target, neighbour_tiles, live_tiles, initial_density, susceptibility, ion_potential,
):
    vmem = pl.BlockSpec(memory_space=pltpu.VMEM)
    smem = pl.BlockSpec(memory_space=pltpu.SMEM)
    atoms = TILES * TILE
    cells = spread_cell[0, 0]
    weights = spread_weight[0, 0]
    packed_rows = 4 * TILES + 8
    send, packed, slot = pl.pallas_call(
        spread_kernel,
        out_shape=(
            jax.ShapeDtypeStruct((ROWS, 16, G), F32),
            jax.ShapeDtypeStruct((packed_rows, TILE), F32),
            jax.ShapeDtypeStruct((1, NLINES), jnp.int32),
        ),
        in_specs=[smem] + [vmem] * 8,
        out_specs=(vmem,) * 3,
        compiler_params=pltpu.CompilerParams(vmem_limit_bytes=VMEM_LIMIT),
        name="spread",
    )(
        live_tiles, cells, weights, atom_charges[0], atom_positions[0, 0].reshape(3, TILES, TILE),
        atom_charges.reshape(TILES, TILE), line_slab[0, 0], line_slab.reshape(1, NLINES),
        line_target[0],
    )
    square, big, flat = (jnp.asarray(table) for table in tables())
    block = initial_density.shape
    dma = pltpu.SemaphoreType.DMA
    potential, density, halo, back = pl.pallas_call(
        field_kernel,
        out_shape=(
            jax.ShapeDtypeStruct(block, F32),
            jax.ShapeDtypeStruct(block, F32),
            jax.ShapeDtypeStruct((9, packed_rows, TILE), F32),
            jax.ShapeDtypeStruct((ROWS, 16, G), F32),
        ),
        in_specs=[vmem] * 8,
        out_specs=(vmem,) * 4,
        scratch_shapes=[
            pltpu.VMEM((ROWS, 16, G), F32),
            pltpu.VMEM((2, G, G), F32),
            pltpu.VMEM((2, G, G), F32),
            pltpu.VMEM((2, G, G), F32),
            pltpu.VMEM((2, G, G), F32),
            pltpu.VMEM((ROWS, G), F32),
            pltpu.VMEM((ROWS, G), F32),
            pltpu.VMEM((2 * ROWS, G), F32),
            pltpu.VMEM((2, 2, 2, 2, 32, G), F32),
            pltpu.VMEM((G, G), F32),
            pltpu.VMEM((ROWS, 16, G), F32),
            pltpu.VMEM((2, G, G), F32),
            dma((2,)),
            dma((2, 3, 3)),
            dma((2, 3)),
            dma((9,)),
            dma((9,)),
            dma((2,)),
            dma((3,)),
            dma((2, 2, 2)),
            dma((2,)),
        ],
        compiler_params=pltpu.CompilerParams(
            collective_id=0, has_side_effects=True, vmem_limit_bytes=VMEM_LIMIT
        ),
        name="field",
    )(send, packed, initial_density, susceptibility, ion_potential, square, big, flat)
    values = pl.pallas_call(
        atom_kernel,
        out_shape=jax.ShapeDtypeStruct((1, atoms), F32),
        in_specs=[smem] * 2 + [vmem] * 6,
        out_specs=vmem,
        scratch_shapes=[
            pltpu.VMEM((3, TILE, TILES), F32),
            pltpu.VMEM((TILE, TILE), F32),
            pltpu.VMEM((1, atoms), F32),
        ],
        compiler_params=pltpu.CompilerParams(vmem_limit_bytes=VMEM_LIMIT),
        name="atoms",
    )(live_tiles, neighbour_tiles[0, 0], halo, back, slot, cells, weights, multipole_basis[0, 0])
    return potential, density, values[None]


def solution(mesh):
    row = ("group", "dom")
    placed = (
        P(row, "pen", None, None),
        P(row, "pen", None),
        P(row, "pen", None, None),
        P(row, "pen", None, None),
        P(row, "pen", None, None),
        P(row, "pen", None, None),
        P(row, "pen", None),
        P(row, "pen", None, None),
        P(row, "pen"),
        P(row, "pen", None),
        P(row, "pen", None),
        P(row, "pen", None),
    )
    return jax.shard_map(
        shards,
        mesh=mesh,
        in_specs=placed,
        out_specs=(P(row, "pen", None), P(row, "pen", None), P(row, "pen", None)),
        check_vma=False,
    )
```

time: 1010 us -> 155 us (0.15)
  the two profiles are of different devices: /device:TPU:1 before, /device:TPU:65 now
where the time goes in v1:
time: 155 us
  Pallas kernels  147 us (95%)
  local copies, waits for them, and re-layouts  6.93 us (4%)
    pallas_call x1, Pallas kernels, shards(): pl.pallas_call(field_kernel, out_shape=(jax.ShapeDtypeStruct(block, F32),...  109 us
    pallas_call x1, Pallas kernels, shards(): pl.pallas_call(atom_kernel, out_shape=jax.ShapeDtypeStruct((1, atoms), F3...  31.6 us
    unnamed x30, local copies, waits for them, and re-layouts  6.8 us
    pallas_call x1, Pallas kernels, shards(): pl.pallas_call(spread_kernel, out_shape=(jax.ShapeDtypeStruct((ROWS, 16,...  6 us

profile of v1, /device:TPU:65, one launch (start us, length us, event | category | flops | bytes accessed | tf_op | source)
XLA Modules:
  0.0 154.8 jit_solution(13121188498482030088)
XLA Ops:
  1.3 0.0 copy-start.13
  1.3 0.0 copy-start.12
  1.3 0.0 copy-start.9
  1.3 0.7 copy-done.12
  2.0 0.0 copy-start.1
  2.0 0.0 copy-start.2
  2.0 0.0 copy-start.3
  2.0 0.1 copy.18.slab_col_ref
  2.1 0.0 copy-done.13
  2.1 0.0 copy-done.9
  2.1 0.7 copy-done.1
  2.8 0.0 copy-done.2
  2.8 0.0 copy-start.10
  2.8 0.7 copy-done.10
  3.6 0.0 copy-start.5
  3.6 6.0 %spread.1 = (f32[64,16,128]{2,1,0:T(8,128)S(1)}, f32[72,128]{1,0:T(8,128)S(1)}, s32[1,256]{1,0:T(1,128)S(1)}) custom-call(s32[1,1]{1,0:T(1,128)S(6)} %copy.21.live_ref, s32[8,2048]{1,0:T(8,128)S(1)} %bitcast.11, f32[8,2048]{1,0:T(8,128)S(1)} %bitcast.13, f32[1,2048]{1,0:T(1,128)S(1)} %bitcast.16, f32[3,16,128]{2,1,0:T(8,128)S(1)} %bitcast.18, ...), custom_call_target="tpu_custom_call" | custom-call | tf_op jit(solution)/shard_map/spread/pallas_call | solution.py:522
  9.6 0.0 copy-done.3
  9.6 0.0 copy-done.5
  9.6 0.0 copy-start
  9.6 1.0 copy-done
  10.7 0.0 copy-start.4
  10.7 0.9 copy-done.4
  11.5 0.0 copy-start.6
  11.5 0.8 copy-done.6
  12.3 0.0 copy-start.7
  12.3 0.8 copy-done.7
  13.1 0.0 copy-start.8
  13.1 0.0 copy-start.11
  13.1 109.0 %field.1 = (f32[2,32,128]{2,1,0:T(8,128)S(1)}, f32[2,32,128]{2,1,0:T(8,128)S(1)}, f32[9,72,128]{2,1,0:T(8,128)S(1)}, f32[64,16,128]{2,1,0:T(8,128)S(1)}) custom-call(f32[64,16,128]{2,1,0:T(8,128)S(1)} %get-tuple-element.10.send_ref, f32[72,128]{1,0:T(8,128)S(1)} %get-tuple-element.11.packed_ref, f32[2,32,128]{2,1,0:T(8,128)S(1)} %copy-done.5, ...), custom_call_target="tpu_custom_call" | custom-call | tf_op jit(solution)/shard_map/field/pallas_call | solution.py:541
  122.0 0.0 copy-done.8
  122.1 0.0 copy-done.11
  122.1 31.6 %atoms.1 = f32[1,2048]{1,0:T(1,128)} custom-call(s32[1,1]{1,0:T(1,128)S(6)} %copy.21.live_ref, s32[16,16]{1,0:T(8,128)S(1)} %bitcast.19, f32[9,72,128]{2,1,0:T(8,128)S(1)} %get-tuple-element.14.halo_ref, f32[64,16,128]{2,1,0:T(8,128)S(1)} %get-tuple-element.15.back_ref, s32[1,256]{1,0:T(1,128)S(1)} %get-tuple-element.16.slot_ref, s32[8,2048]{1,0:T(8,128)S(1)} %bitcast.12, ...), custom_call_target="tpu_custom_call" | custom-call | tf_op jit(solution)/shard_map/atoms/pallas_call | solution.py:579
  153.6 0.6 copy.22
  154.2 0.6 copy.23
Async XLA Ops:
  1.3 0.8 copy-start.13
  1.3 0.7 copy-start.12
  1.3 0.8 copy-start.9
  2.0 0.8 copy-start.1
  2.0 0.9 copy-start.2
  2.0 7.6 %copy-start.3 = (bf16[8,128,128]{2,1,0:T(8,128)(2,1)S(1)}, bf16[8,128,128]{2,1,0:T(8,128)(2,1)}, u32[]{:S(2)}) copy-start(bf16[8,128,128]{2,1,0:T(8,128)(2,1)} %constant.6.clone.square_ref) | copy-start | bytes 786436
  2.8 0.7 copy-start.10
  3.6 6.0 %copy-start.5 = (f32[2,32,128]{2,1,0:T(8,128)S(1)}, f32[2,32,128]{2,1,0:T(8,128)}, u32[]{:S(2)}) copy-start(f32[2,32,128]{2,1,0:T(8,128)} %rho_ref.1) | copy-start | bytes 98308
  9.6 1.0 copy-start
  10.7 0.9 copy-start.4
  11.5 0.8 copy-start.6
  12.3 0.8 copy-start.7
  13.1 109.0 %copy-start.8 = (f32[1,1,4,2048]{3,2,1,0:T(4,128)S(1)}, f32[1,1,4,2048]{3,2,1,0:T(4,128)}, u32[]{:S(2)}) copy-start(f32[1,1,4,2048]{3,2,1,0:T(4,128)} %param.17) | copy-start | bytes 98308
  13.1 109.0 %copy-start.11 = (s32[1,1,16,16]{3,2,1,0:T(8,128)S(1)}, s32[1,1,16,16]{3,2,1,0:T(8,128)}, u32[]{:S(2)}) copy-start(s32[1,1,16,16]{3,2,1,0:T(8,128)} %param.22) | copy-start | bytes 3076

commit v2 on v1

v2 whole, which is shorter than its diff:
```python
import math

import jax
import jax.numpy as jnp
import ml_dtypes
import numpy as np
from jax import lax
from jax.experimental import pallas as pl
from jax.experimental.pallas import tpu as pltpu
from jax.sharding import PartitionSpec as P

MESH = pl.DeviceIdType.MESH
F32 = jnp.float32
BF16 = jnp.bfloat16
G = 128
TILE = 128
TILES = 16
NBR = 16
ITERS = 4
ROWS = 64
PEN = 4
CAP = 8
NLINES = 256
MIX_RATE = 0.3
SCREENING = 0.1
BOX_HEIGHT = 4.0
SOFTENING = 0.01
ERF_SHIFT = 1.35
ERF_POLY = (
    8.048848463632075e-05,
    0.279831566396696,
    0.40782855654035,
    0.3006583844815809,
    1.260144403309312,
    -1.158323294058104,
    2.9062706842895354,
    -1.262709002135607,
)
VMEM_LIMIT = 64 * 1024 * 1024


def halves(table):
    high = table.astype(ml_dtypes.bfloat16)
    low = (table - high.astype(np.float64)).astype(ml_dtypes.bfloat16)
    return [high, low]


def tables():
    k = np.arange(G)
    angle = 2.0 * np.pi * (np.outer(k, k) % G) / G
    cas = (np.cos(angle) + np.sin(angle)) / np.sqrt(G)
    order = np.concatenate([np.arange(32) + 32 * (2 * z + c) for c in range(2) for z in range(2)])
    split_x = np.concatenate([np.arange(ROWS) * 2, np.arange(ROWS) * 2 + 1])
    square = halves(cas) + halves(cas[:, order]) + halves(cas[:, split_x]) + halves(cas[split_x, :])
    wide = np.zeros((2, G, 2, 2, ROWS))
    for x in range(2):
        for h in range(2):
            wide[x, :, h, x, :] = cas[:, h * ROWS : (h + 1) * ROWS]
    wide = wide.reshape(2 * G, 2 * G)
    big = halves(wide) + halves(wide.T)
    lam = 2.0 - 2.0 * np.cos(2.0 * np.pi * k / G)
    lam_rows = np.repeat(lam[:, None], G, axis=1)
    lam_lanes = np.zeros((8, G))
    for h in range(2):
        lam_lanes[h] = np.tile(lam[h * ROWS : (h + 1) * ROWS], 2)
    flat = np.concatenate([lam_rows, lam_lanes]).astype(np.float32)
    big = [part[:, h * G : (h + 1) * G] for part in big for h in range(2)]
    return np.stack(square), np.stack(big), flat


def split(x):
    high = x.astype(BF16)
    return high, (x - high.astype(F32)).astype(BF16)


def dot(a, b):
    return jnp.dot(a, b, preferred_element_type=F32)


def dot_nt(a, b):
    return lax.dot_general(a, b, (((1,), (1,)), ((), ())), preferred_element_type=F32)


def dot_tn(a, b):
    return lax.dot_general(a, b, (((0,), (0,)), ((), ())), preferred_element_type=F32)


def left_const(high, low, x):
    x_high, x_low = split(x)
    return dot(high, x_high) + (dot(high, x_low) + dot(low, x_high))


def right_const(x, high, low):
    x_high, x_low = split(x)
    return dot(x_high, high) + (dot(x_low, high) + dot(x_high, low))


def iota(shape, dim):
    return lax.broadcasted_iota(jnp.int32, shape, dim)


CHUNK = 512
FWD_TILES = 2
RET_TILES = 1


def pair_values(own, partner):
    dx = own[0] - partner[0]
    dy = own[1] - partner[1]
    dz = own[2] - partner[2]
    s = dx * dx + dy * dy + dz * dz + SOFTENING
    u = lax.rsqrt(s)
    t = 1.0 / (s * u + ERF_SHIFT)
    poly = jnp.full_like(t, ERF_POLY[-1])
    for coefficient in ERF_POLY[-2::-1]:
        poly = poly * t + coefficient
    return (partner[3] * u) * (poly * jnp.exp(-4.0 * s))


def kernel(
    live_ref, nbr_ref, cell_hbm, weight_hbm, positions_hbm, charge_hbm, slab_hbm, target_hbm,
    rho_hbm, sus_hbm, ion_hbm, basis_hbm, square_hbm, big_hbm, flat_hbm,
    pot_out, rho_out, mm_out,
    cells, weights, charges, slab_buf, target_buf, basis_ref, square_ref, big_ref, flat_ref,
    send_ref, line_buf, halo_ref, mm, rho, sus, ion, fwd_send, fwd_recv, ret_send, ret_recv,
    green, line_send, last_pot, back_ref, columns_of, short,
    load_sems, line_sems, pen_sems, mm_sems, halo_send_sems, halo_recv_sems, fwd_sems, ret_sems,
    core_sems, back_sems,
):
    group, dom, pen = lax.axis_index("group"), lax.axis_index("dom"), lax.axis_index("pen")
    me = group * 16 + dom
    core, z_lo = lax.rem(pen, 2), pen // 2
    other_chip = lax.rem(pen + 2, PEN)
    sibling = z_lo * 2 + (1 - core)
    columns = pl.ds(pl.multiple_of(pen * 32, 32), 32)
    live = live_ref[0, 0]

    first = [
        pltpu.make_async_copy(source, target, load_sems.at[index])
        for index, (source, target) in enumerate(
            (
                (cell_hbm, cells),
                (weight_hbm, weights),
                (charge_hbm, charges),
                (slab_hbm, slab_buf),
                (target_hbm, target_buf),
                (positions_hbm, halo_ref.at[4, pl.ds(0, 3 * TILES)]),
            )
        )
    ]
    later = [
        pltpu.make_async_copy(source, target, load_sems.at[6 + index])
        for index, (source, target) in enumerate(
            (
                (rho_hbm, rho.at[:, columns, :]),
                (sus_hbm, sus.at[:, columns, :]),
                (ion_hbm, ion.at[:, columns, :]),
                (flat_hbm, flat_ref),
                (square_hbm, square_ref),
                (big_hbm, big_ref),
                (basis_hbm, basis_ref),
            )
        )
    ]
    for copy in first + later:
        copy.start()

    def device(row, column):
        return (row // 16, lax.rem(row, 16), column)

    def remote(src, dst, send_sem, recv_sem, row, column):
        return pltpu.make_async_remote_copy(
            src_ref=src, dst_ref=dst, send_sem=send_sem, recv_sem=recv_sem,
            device_id=device(row, column), device_id_type=MESH,
        )

    def ring(q):
        return lax.rem(2 + 3 * q + (q // 2) * (2 * q - 1), 4)

    def peer(k):
        far_group = lax.rem(group + ring(k // 16), 4)
        far_x = lax.rem(dom // 4 + ring(lax.rem(k // 4, 4)), 4)
        far_y = lax.rem(lax.rem(dom, 4) + ring(lax.rem(k, 4)), 4)
        return far_group * 16 + far_x * 4 + far_y

    barrier = pltpu.get_barrier_semaphore()

    def greet(k, carry):
        row = peer(k)
        pl.semaphore_signal(barrier, inc=1, device_id=device(row, pen), device_id_type=MESH)
        pl.semaphore_signal(barrier, inc=1, device_id=device(row, other_chip), device_id_type=MESH)
        return carry

    lax.fori_loop(0, ROWS - 1, greet, 0)
    for k in (1, 2, 3):
        pl.semaphore_signal(
            barrier, inc=1, device_id=device(me, lax.rem(pen + k, PEN)), device_id_type=MESH
        )
    for dx in (1, ROWS - 1):
        for dy in (1, PEN - 1):
            pl.semaphore_signal(
                barrier, inc=1, device_id=device(lax.rem(me + dx, ROWS), lax.rem(pen + dy, PEN)),
                device_id_type=MESH,
            )

    for copy in first:
        copy.wait()
    halo_ref[4, 3 * TILES :, :] = jnp.where(iota((TILES, TILE), 0) < live, charges[...], 0.0)
    slab_row = slab_buf[...]
    slab_rows = slab_row.astype(F32)
    slab_cols = jnp.concatenate(
        [
            jnp.broadcast_to(slab_rows[:, half * G : (half + 1) * G], (G, G)).T
            for half in range(2)
        ],
        axis=0,
    )
    slab_cols = jnp.concatenate([slab_cols, slab_cols], axis=1)
    same = (slab_cols == slab_rows) & (iota((NLINES, NLINES), 0) < iota((NLINES, NLINES), 1))
    rank = jnp.sum(same.astype(F32), axis=0, keepdims=True).astype(jnp.int32)
    pick = (iota((ROWS * CAP, NLINES), 0) == slab_row * CAP + rank).astype(F32).astype(BF16)
    owner = jnp.where(iota((ROWS, NLINES), 0) == slab_row, target_buf[...].astype(F32), 0.0)
    place = (iota((TILE, NLINES), 0) == rank).astype(F32)
    line_iota = iota((NLINES, CHUNK), 0)
    cell_iota = iota((G, CHUNK), 0)

    def spread(chunk, total):
        where = pl.ds(pl.multiple_of(chunk * CHUNK, CHUNK), CHUNK)
        charge = jnp.concatenate(
            [
                halo_ref[4, pl.ds(3 * TILES + chunk * (CHUNK // TILE) + q, 1), :]
                for q in range(CHUNK // TILE)
            ],
            axis=1,
        )
        for corner in range(8):
            cell = cells[corner : corner + 1, where]
            high, low = split(weights[corner : corner + 1, where] * charge)
            hit = line_iota == cell // G
            lines = jnp.concatenate(
                [
                    jnp.where(hit, high.astype(F32), 0.0).astype(BF16),
                    jnp.where(hit, low.astype(F32), 0.0).astype(BF16),
                ],
                axis=0,
            )
            spots = (cell_iota == cell % G).astype(F32).astype(BF16)
            total = total + dot_nt(lines, spots)
        return total

    total = lax.fori_loop(0, TILES * TILE // CHUNK, spread, jnp.zeros((2 * NLINES, G), F32))
    lines_high, lines_low = split(total[:NLINES] + total[NLINES:])
    send_ref[:, :CAP, :] = (dot(pick, lines_high) + dot(pick, lines_low)).reshape(ROWS, CAP, G)
    send_ref[:, CAP, :] = dot_nt(owner.astype(BF16), place.astype(BF16))

    pl.semaphore_wait(barrier, 2 * (ROWS - 1) + 3 + 4)

    def send_lines(k, carry):
        row = peer(k)
        remote(
            send_ref.at[row, pl.ds(0, CAP + 1)], line_buf.at[me, pl.ds(0, CAP + 1)],
            line_sems.at[0], line_sems.at[1], row, pen,
        ).start()
        return carry

    lax.fori_loop(0, ROWS - 1, send_lines, 0)
    line_buf[me, 0 : CAP + 1, :] = send_ref[me, 0 : CAP + 1, :]

    slabs = ((rho_hbm, rho), (sus_hbm, sus), (ion_hbm, ion))

    def slab_copy(index, k):
        source, whole = slabs[index]
        return remote(
            source, whole.at[:, columns, :],
            pen_sems.at[0, index, k - 1], pen_sems.at[1, index, k - 1],
            me, lax.rem(pen + k, PEN),
        )

    for k in (1, 2, 3):
        slab_copy(0, k).start()

    neighbours = [(dx, dy) for dx in (-1, 0, 1) for dy in (-1, 0, 1) if (dx, dy) != (0, 0)]

    def halo_copy(dx, dy):
        number = (1 - dx) * 3 + 1 - dy
        return remote(
            halo_ref.at[4], halo_ref.at[number], halo_send_sems.at[number],
            halo_recv_sems.at[number],
            lax.rem(me + dx + ROWS, ROWS), lax.rem(pen + dy + PEN, PEN),
        )

    for dx, dy in neighbours:
        halo_copy(dx, dy).start()
    for copy in later:
        copy.wait()

    half = me // 32
    y_row = pen * 32 + lax.rem(me, 32)
    lam_yz = flat_ref[pl.ds(y_row, 1), :] + flat_ref[pl.ds(G + half, 1), :]
    green[...] = 1.0 / (SCREENING + (flat_ref[0:G, :] + lam_yz))

    source_of = iota((ROWS * CAP, ROWS), 0) // CAP == iota((ROWS * CAP, ROWS), 1)
    source_of = source_of.astype(F32).astype(BF16)
    own_lane = iota((ROWS * CAP, G), 1) == lax.rem(iota((ROWS * CAP, G), 0), CAP)
    for axis in range(3):
        columns_of[axis] = halo_ref[4, axis * TILES : (axis + 1) * TILES, :].T * (
            BOX_HEIGHT if axis == 2 else 1.0
        )

    def whole_line_copy(ref, sems):
        most = ref.at[pl.ds(0, ROWS - 1), pl.ds(0, CAP + 1)]
        return pltpu.make_async_remote_copy(
            src_ref=most, dst_ref=most, send_sem=sems.at[0], recv_sem=sems.at[1],
            device_id=device(lax.rem(me + 1, ROWS), pen), device_id_type=MESH,
        )

    whole_line_copy(line_buf, line_sems).wait_recv()
    spread_targets = dot(source_of, line_buf[:, CAP, :].astype(BF16))
    target = jnp.sum(jnp.where(own_lane, spread_targets, 0.0), axis=1, keepdims=True)
    landing = (target == iota((ROWS * CAP, ROWS), 1).astype(F32)).astype(F32)
    landing_t = landing.T.astype(BF16)
    landing = landing.astype(BF16)
    lines_high, lines_low = split(line_buf[:, :CAP, :].reshape(ROWS * CAP, G))
    own_mm = dot(landing_t, lines_high) + dot(landing_t, lines_low)
    for x in range(2):
        mm[x, columns, :] = own_mm[x * 32 : (x + 1) * 32]

    def mm_copy(k):
        return remote(
            mm.at[:, columns, :], mm.at[:, columns, :], mm_sems.at[0, k - 1], mm_sems.at[1, k - 1],
            me, lax.rem(pen + k, PEN),
        )

    for k in (1, 2, 3):
        mm_copy(k).start()
    for k in (1, 2, 3):
        slab_copy(0, k).wait_recv()
    for k in (1, 2, 3):
        mm_copy(k).wait_recv()

    tile_lane = iota((TILE, TILES), 1)

    def own_tile(t, carry):
        own = [
            jnp.broadcast_to(
                jnp.sum(jnp.where(tile_lane == t, columns_of[axis], 0.0), axis=1, keepdims=True),
                (TILE, TILE),
            )
            for axis in range(3)
        ]

        def partner_tile(n, total):
            chosen = nbr_ref[t, n]
            d = lax.div(chosen, TILES)
            tile = lax.rem(chosen, TILES)
            row = [halo_ref[d, pl.ds(axis * TILES + tile, 1), :] for axis in range(4)]
            row[0] = row[0] + (lax.div(d, 3) - 1).astype(F32)
            row[1] = row[1] + (lax.rem(d, 3) - 1).astype(F32)
            row[2] = row[2] * BOX_HEIGHT
            return total + pair_values(own, row)

        total = lax.fori_loop(0, NBR, partner_tile, jnp.zeros((TILE, TILE), F32))
        short[:, pl.ds(pl.multiple_of(t * TILE, TILE), TILE)] = jnp.sum(
            total.T, axis=0, keepdims=True
        )
        return carry

    def wide(index):
        return jnp.concatenate([big_ref[2 * index], big_ref[2 * index + 1]], axis=1)

    done = 0
    low_lanes = iota((ROWS, G), 1) < ROWS

    def fwd_all():
        most_send, most_recv = fwd_send.at[pl.ds(0, ROWS - 1)], fwd_recv.at[pl.ds(0, ROWS - 1)]
        return pltpu.make_async_remote_copy(
            src_ref=most_send, dst_ref=most_recv, send_sem=fwd_sems.at[0], recv_sem=fwd_sems.at[1],
            device_id=device(lax.rem(me + 1, ROWS), pen), device_id_type=MESH,
        )

    def ret_copy(slot, row, column):
        return remote(
            ret_send.at[pl.ds(row, 1)],
            ret_recv.at[slot, half, core, z_lo, pl.ds(lax.rem(me, 32), 1)],
            ret_sems.at[0], ret_sems.at[1 + slot], row, column,
        )

    def ret_all(slot):
        most = ret_send.at[pl.ds(0, 2 * ROWS - 1)]
        return pltpu.make_async_remote_copy(
            src_ref=most, dst_ref=most, send_sem=ret_sems.at[0], recv_sem=ret_sems.at[1 + slot],
            device_id=device(lax.rem(me + 1, ROWS), pen), device_id_type=MESH,
        )

    def core_copy(slot, h):
        return remote(
            ret_recv.at[slot, h, core], ret_recv.at[slot, h, core],
            core_sems.at[0, slot, h], core_sems.at[1, slot, h], me, sibling,
        )

    for iteration in range(ITERS):
        slot = iteration % 2
        source = jnp.concatenate([rho[0] + mm[0], rho[1] + mm[1]], axis=1)
        spectrum = left_const(square_ref[0, columns, :], square_ref[1, columns, :], source)
        spectrum = right_const(spectrum, wide(0), wide(1))
        if iteration > 0:
            fwd_all().wait_send()
        fwd_send[0:32, :] = spectrum[:, :G]
        fwd_send[32:64, :] = spectrum[:, G:]

        def send_fwd(k, carry):
            row = peer(k)
            remote(
                fwd_send.at[pl.ds(row, 1)], fwd_recv.at[pl.ds(me, 1)],
                fwd_sems.at[0], fwd_sems.at[1], row, pen,
            ).start()
            return carry

        lax.fori_loop(0, ROWS - 1, send_fwd, 0)
        fwd_recv[pl.ds(me, 1), :] = fwd_send[pl.ds(me, 1), :]
        if iteration == 0:
            for index in (1, 2):
                for k in (1, 2, 3):
                    slab_copy(index, k).start()
            for dx, dy in neighbours:
                halo_copy(dx, dy).wait()
            for dx, dy in neighbours:
                outside = (me + dx < 0) | (me + dx >= ROWS) | (pen + dy < 0) | (pen + dy >= PEN)

                @pl.when(outside)
                def _():
                    halo_ref[(dx + 1) * 3 + dy + 1] = jnp.zeros((4 * TILES, TILE), F32)

        lax.fori_loop(done, done + FWD_TILES, own_tile, 0)
        done += FWD_TILES
        fwd_all().wait_recv()
        received = fwd_recv[...]
        both = jnp.concatenate([received, pltpu.roll(received, ROWS, 1)], axis=0)
        modes = left_const(square_ref[4], square_ref[5], both) * green[...]
        solved = left_const(square_ref[6], square_ref[7], modes)
        if iteration > 0:
            ret_all(1 - slot).wait_send()
        ret_send[:ROWS, :] = jnp.where(low_lanes, solved[:ROWS], pltpu.roll(solved[ROWS:], ROWS, 1))

        def send_ret(k, carry):
            row = peer(k)
            ret_copy(slot, row, other_chip).start()
            ret_copy(slot, row, pen).start()
            return carry

        lax.fori_loop(0, ROWS - 1, send_ret, 0)
        ret_copy(slot, me, other_chip).start()
        ret_recv[slot, half, core, z_lo, pl.ds(lax.rem(me, 32), 1)] = ret_send[pl.ds(me, 1), :]
        lax.fori_loop(done, done + RET_TILES, own_tile, 0)
        done += RET_TILES
        ret_all(slot).wait_recv()
        for h in range(2):
            core_copy(slot, h).start()
        if iteration == 0:
            for index in (1, 2):
                for k in (1, 2, 3):
                    slab_copy(index, k).wait_recv()
        for h in range(2):
            core_copy(slot, h).wait_recv()
        lines = jnp.concatenate([ret_recv[slot, h].reshape(G, G) for h in range(2)], axis=1)
        lines = right_const(lines, wide(2), wide(3))
        potential = left_const(square_ref[2], square_ref[3], lines)
        for x in range(2):
            own = potential[:, x * G : (x + 1) * G]
            if iteration == ITERS - 1:
                last_pot[x] = own
            rho[x] = rho[x] - MIX_RATE * (rho[x] + sus[x] * (own + ion[x]))
        for h in range(2):
            core_copy(slot, h).wait_send()

    row_u = 1.0 + 2.0 * (iota((G, G), 0).astype(F32) + 0.5) / G
    lane_u = 1.0 + 2.0 * (iota((G, G), 1).astype(F32) + 0.5) / G
    x_u = [1.0 + 2.0 * ((2 * me + x).astype(F32) + 0.5) / G for x in range(2)]
    weighted = rho[0] * x_u[0] + rho[1] * x_u[1]
    plain = rho[0] + rho[1]
    sums = [weighted, plain * row_u, weighted * row_u, plain * lane_u]
    own_moments = jnp.zeros((1, G), F32)
    for index, term in enumerate(sums):
        value = jnp.sum(jnp.sum(term, axis=0, keepdims=True), axis=1, keepdims=True)
        own_moments = jnp.where(iota((1, G), 1) == index, value, own_moments)
    own_pot = jnp.concatenate([last_pot[x, columns, :] for x in range(2)], axis=0)
    pot_high, pot_low = split(own_pot)
    line_send[:, :CAP, :] = (dot(landing, pot_high) + dot(landing, pot_low)).reshape(ROWS, CAP, G)
    line_send[:, CAP, :] = jnp.broadcast_to(own_moments, (ROWS, G))

    def send_back(k, carry):
        row = peer(k)
        remote(
            line_send.at[row, pl.ds(0, CAP + 1)], back_ref.at[me, pl.ds(0, CAP + 1)],
            back_sems.at[0], back_sems.at[1], row, pen,
        ).start()
        return carry

    lax.fori_loop(0, ROWS - 1, send_back, 0)
    back_ref[me, 0 : CAP + 1, :] = line_send[me, 0 : CAP + 1, :]
    for x in range(2):
        pot_out[x] = last_pot[x, columns, :]
        rho_out[x] = rho[x, columns, :]
    lax.fori_loop(done, TILES, own_tile, 0)

    whole_line_copy(line_buf, line_sems).wait_send()
    for k in (1, 2, 3):
        for index in range(3):
            slab_copy(index, k).wait_send()
        mm_copy(k).wait_send()
    fwd_all().wait_send()
    ret_all((ITERS - 1) % 2).wait_send()
    whole_line_copy(line_send, back_sems).wait()

    back_high, back_low = split(back_ref[:, :CAP, :].reshape(ROWS * CAP, G))
    values = dot_tn(jnp.concatenate([back_high, back_low], axis=1), pick)
    values_high, values_low = split(values[:G] + values[G:])
    values = jnp.concatenate([values_high, values_low], axis=0)
    moments = jnp.sum(back_ref[:, CAP, :], axis=0, keepdims=True) * (1.0 / (G * math.sqrt(G)))
    moment = [
        jnp.sum(jnp.where(iota((1, G), 1) == m, moments, 0.0), axis=1, keepdims=True)
        for m in range(4)
    ]

    def gather(chunk, carry):
        where = pl.ds(pl.multiple_of(chunk * CHUNK, CHUNK), CHUNK)
        total = short[:, where]
        for corner in range(8):
            cell = cells[corner : corner + 1, where]
            lines = (line_iota == cell // G).astype(F32).astype(BF16)
            found = dot(values, lines)
            found = jnp.where(cell_iota == cell % G, found[:G] + found[G:], 0.0)
            total = total + weights[corner : corner + 1, where] * jnp.sum(
                found, axis=0, keepdims=True
            )
        for m in range(4):
            total = total + moment[m] * basis_ref[m : m + 1, where]
        atom = chunk * CHUNK + iota((1, CHUNK), 1)
        mm_out[:, where] = jnp.where(atom // TILE < live, total, 0.0)
        return carry

    lax.fori_loop(0, TILES * TILE // CHUNK, gather, 0)


def shards(
    atom_positions, atom_charges, multipole_basis, spread_cell, spread_weight, line_slab,
    line_target, neighbour_tiles, live_tiles, initial_density, susceptibility, ion_potential,
):
    vmem = pl.BlockSpec(memory_space=pltpu.VMEM)
    smem = pl.BlockSpec(memory_space=pltpu.SMEM)
    hbm = pl.BlockSpec(memory_space=pltpu.HBM)
    atoms = TILES * TILE
    square, big, flat = (jnp.asarray(table) for table in tables())
    block = initial_density.shape
    dma = pltpu.SemaphoreType.DMA
    buffer = pltpu.VMEM
    potential, density, values = pl.pallas_call(
        kernel,
        out_shape=(
            jax.ShapeDtypeStruct(block, F32),
            jax.ShapeDtypeStruct(block, F32),
            jax.ShapeDtypeStruct((1, atoms), F32),
        ),
        in_specs=[smem] * 2 + [hbm] * 13,
        out_specs=(vmem,) * 3,
        scratch_shapes=[
            buffer((8, atoms), jnp.int32),
            buffer((8, atoms), F32),
            buffer((TILES, TILE), F32),
            buffer((1, NLINES), jnp.int32),
            buffer((1, NLINES), jnp.int32),
            buffer((4, atoms), F32),
            buffer(square.shape, BF16),
            buffer(big.shape, BF16),
            buffer(flat.shape, F32),
            buffer((ROWS, 16, G), F32),
            buffer((ROWS, 16, G), F32),
            buffer((9, 4 * TILES, TILE), F32),
            buffer((2, G, G), F32),
            buffer((2, G, G), F32),
            buffer((2, G, G), F32),
            buffer((2, G, G), F32),
            buffer((ROWS, G), F32),
            buffer((ROWS, G), F32),
            buffer((2 * ROWS, G), F32),
            buffer((2, 2, 2, 2, 32, G), F32),
            buffer((G, G), F32),
            buffer((ROWS, 16, G), F32),
            buffer((2, G, G), F32),
            buffer((ROWS, 16, G), F32),
            buffer((3, TILE, TILES), F32),
            buffer((1, atoms), F32),
            dma((13,)),
            dma((2,)),
            dma((2, 3, 3)),
            dma((2, 3)),
            dma((9,)),
            dma((9,)),
            dma((2,)),
            dma((3,)),
            dma((2, 2, 2)),
            dma((2,)),
        ],
        compiler_params=pltpu.CompilerParams(
            collective_id=0, has_side_effects=True, vmem_limit_bytes=VMEM_LIMIT
        ),
        name="embed",
    )(
        live_tiles, neighbour_tiles[0, 0], spread_cell[0, 0], spread_weight[0, 0],
        atom_positions.reshape(3 * TILES, TILE), atom_charges.reshape(TILES, TILE),
        line_slab.reshape(1, NLINES), line_target[0], initial_density, susceptibility,
        ion_potential, multipole_basis[0, 0], square, big, flat,
    )
    return potential, density, values[None]


def solution(mesh):
    row = ("group", "dom")
    placed = (
        P(row, "pen", None, None),
        P(row, "pen", None),
        P(row, "pen", None, None),
        P(row, "pen", None, None),
        P(row, "pen", None, None),
        P(row, "pen", None, None),
        P(row, "pen", None),
        P(row, "pen", None, None),
        P(row, "pen"),
        P(row, "pen", None),
        P(row, "pen", None),
        P(row, "pen", None),
    )
    return jax.shard_map(
        shards,
        mesh=mesh,
        in_specs=placed,
        out_specs=(P(row, "pen", None), P(row, "pen", None), P(row, "pen", None)),
        check_vma=False,
    )
```

time: 155 us -> 128 us (0.83)
  the two profiles are of different devices: /device:TPU:65 before, /device:TPU:1 now
where the time goes in v2:
time: 128 us
  Pallas kernels  124 us (97%)
  local copies, waits for them, and re-layouts  2.69 us (2%)
  between operations  1.3 us (1%)
    pallas_call x1, Pallas kernels, shards(): pl.pallas_call(kernel, out_shape=(jax.ShapeDtypeStruct(block, F32), jax.S...  124 us
    unnamed x7, local copies, waits for them, and re-layouts  2.69 us

profile of v2, /device:TPU:1, one launch (start us, length us, event | category | flops | bytes accessed | tf_op | source)
XLA Modules:
  0.0 128.1 jit_solution(30966167066407137)
XLA Ops:
  1.3 124.1 %embed.1 = (f32[2,32,128]{2,1,0:T(8,128)}, f32[2,32,128]{2,1,0:T(8,128)}, f32[1,2048]{1,0:T(1,128)}) custom-call(s32[1,1]{1,0:T(1,128)S(6)} %copy.21.live_ref, s32[16,16]{1,0:T(8,128)} %bitcast.13, s32[8,2048]{1,0:T(8,128)} %bitcast.9, f32[8,2048]{1,0:T(8,128)} %bitcast.10, f32[48,128]{1,0:T(8,128)} %bitcast.12, f32[16,128]{1,0:T(8,128)} %bitcast.14, ...), custom_call_target="tpu_custom_call" | custom-call | tf_op jit(solution)/shard_map/embed/pallas_call | solution.py:557
  125.4 0.0 copy-start
  125.4 1.4 %copy.22 = f32[2,32,128]{2,1,0:T(8,128)} copy(f32[2,32,128]{2,1,0:T(8,128)} %get-tuple-element.12) | data formatting | bytes 65536
  126.8 0.0 copy-done
  126.8 0.0 copy-start.1
  126.8 0.6 copy.23
  127.4 0.1 copy-done.1
  127.5 0.6 copy.24
Async XLA Ops:
  125.4 1.4 %copy-start = (f32[2,32,128]{2,1,0:T(8,128)S(1)}, f32[2,32,128]{2,1,0:T(8,128)}, u32[]{:S(2)}) copy-start(f32[2,32,128]{2,1,0:T(8,128)} %get-tuple-element.13) | copy-start | bytes 98308
  126.8 0.7 copy-start.1

commit v3 on v2

--- a/solution.py
+++ b/solution.py
@@ -85,21 +85,25 @@
     return lax.dot_general(a, b, (((0,), (0,)), ((), ())), preferred_element_type=F32)
 
 
-def left_const(high, low, x):
+def left_const(both, x):
+    rows = both.shape[0] // 2
     x_high, x_low = split(x)
-    return dot(high, x_high) + (dot(high, x_low) + dot(low, x_high))
+    wide = dot(both, x_high)
+    return wide[:rows] + (wide[rows:] + dot(both[:rows], x_low))
 
 
 def right_const(x, high, low):
+    rows = x.shape[0]
     x_high, x_low = split(x)
-    return dot(x_high, high) + (dot(x_low, high) + dot(x_high, low))
+    wide = dot(jnp.concatenate([x_high, x_low], axis=0), high)
+    return wide[:rows] + (wide[rows:] + dot(x_high, low))
 
 
 def iota(shape, dim):
     return lax.broadcasted_iota(jnp.int32, shape, dim)
 
 
-CHUNK = 512
+AGREE_TILES = 1
 FWD_TILES = 2
 RET_TILES = 1
 
@@ -123,9 +127,9 @@
     pot_out, rho_out, mm_out,
     cells, weights, charges, slab_buf, target_buf, basis_ref, square_ref, big_ref, flat_ref,
     send_ref, line_buf, halo_ref, mm, rho, sus, ion, fwd_send, fwd_recv, ret_send, ret_recv,
-    green, line_send, last_pot, back_ref, columns_of, short,
+    green, line_send, moment_send, moment_recv, back_ref, columns_of, short,
     load_sems, line_sems, pen_sems, mm_sems, halo_send_sems, halo_recv_sems, fwd_sems, ret_sems,
-    core_sems, back_sems,
+    core_sems, back_sems, moment_sems,
 ):
     group, dom, pen = lax.axis_index("group"), lax.axis_index("dom"), lax.axis_index("pen")
     me = group * 16 + dom
@@ -134,6 +138,7 @@
     sibling = z_lo * 2 + (1 - core)
     columns = pl.ds(pl.multiple_of(pen * 32, 32), 32)
     live = live_ref[0, 0]
+    atoms = TILES * TILE
 
     first = [
         pltpu.make_async_copy(source, target, load_sems.at[index])
@@ -162,46 +167,61 @@
             )
         )
     ]
-    for copy in first + later:
+    for copy in first:
         copy.start()
 
-    def device(row, column):
-        return (row // 16, lax.rem(row, 16), column)
-
-    def remote(src, dst, send_sem, recv_sem, row, column):
+    def remote(src, dst, send_sem, recv_sem, where):
         return pltpu.make_async_remote_copy(
             src_ref=src, dst_ref=dst, send_sem=send_sem, recv_sem=recv_sem,
-            device_id=device(row, column), device_id_type=MESH,
+            device_id=where, device_id_type=MESH,
         )
 
     def ring(q):
         return lax.rem(2 + 3 * q + (q // 2) * (2 * q - 1), 4)
 
-    def peer(k):
-        far_group = lax.rem(group + ring(k // 16), 4)
-        far_x = lax.rem(dom // 4 + ring(lax.rem(k // 4, 4)), 4)
-        far_y = lax.rem(lax.rem(dom, 4) + ring(lax.rem(k, 4)), 4)
-        return far_group * 16 + far_x * 4 + far_y
+    dom_x, dom_y = dom // 4, lax.rem(dom, 4)
+    ys = [lax.rem(dom_y + offset, 4) for offset in (2, 1, 3, 0)]
+
+    def each_x(count, act):
+        def step(q, carry):
+            far_x = lax.rem(dom_x + ring(q), 4) * 4
+            for y in ys:
+                act(far_x + y)
+            return carry
+
+        lax.fori_loop(0, count, step, 0)
+
+    def each_peer(act):
+        def step(q, carry):
+            far_group = lax.rem(group + ring(q // 4), 4)
+            far_x = lax.rem(dom_x + ring(lax.rem(q, 4)), 4) * 4
+            for y in ys:
+                act(far_group, far_x + y)
+            return carry
+
+        lax.fori_loop(0, 15, step, 0)
+        for y in ys[:3]:
+            act(group, dom_x * 4 + y)
 
     barrier = pltpu.get_barrier_semaphore()
 
-    def greet(k, carry):
-        row = peer(k)
-        pl.semaphore_signal(barrier, inc=1, device_id=device(row, pen), device_id_type=MESH)
-        pl.semaphore_signal(barrier, inc=1, device_id=device(row, other_chip), device_id_type=MESH)
-        return carry
-
-    lax.fori_loop(0, ROWS - 1, greet, 0)
+    def signal(*where):
+        pl.semaphore_signal(barrier, inc=1, device_id=where, device_id_type=MESH)
+
+    def greet(far_group, far_dom):
+        signal(far_group, far_dom, pen)
+        signal(far_group, far_dom, other_chip)
+
+    each_peer(greet)
     for k in (1, 2, 3):
-        pl.semaphore_signal(
-            barrier, inc=1, device_id=device(me, lax.rem(pen + k, PEN)), device_id_type=MESH
-        )
+        signal(group, dom, lax.rem(pen + k, PEN))
     for dx in (1, ROWS - 1):
         for dy in (1, PEN - 1):
-            pl.semaphore_signal(
-                barrier, inc=1, device_id=device(lax.rem(me + dx, ROWS), lax.rem(pen + dy, PEN)),
-                device_id_type=MESH,
-            )
+            row = lax.rem(me + dx, ROWS)
+            signal(row // 16, lax.rem(row, 16), lax.rem(pen + dy, PEN))
+
+    for copy in later:
+        copy.start()
 
     for copy in first:
         copy.wait()
@@ -218,52 +238,45 @@
     slab_cols = jnp.concatenate([slab_cols, slab_cols], axis=1)
     same = (slab_cols == slab_rows) & (iota((NLINES, NLINES), 0) < iota((NLINES, NLINES), 1))
     rank = jnp.sum(same.astype(F32), axis=0, keepdims=True).astype(jnp.int32)
-    pick = (iota((ROWS * CAP, NLINES), 0) == slab_row * CAP + rank).astype(F32).astype(BF16)
+    pick = (iota((ROWS * CAP, NLINES), 0) == slab_row * CAP + rank).astype(F32)
+    pick, pick_t = pick.astype(BF16), pick.T.astype(BF16)
     owner = jnp.where(iota((ROWS, NLINES), 0) == slab_row, target_buf[...].astype(F32), 0.0)
     place = (iota((TILE, NLINES), 0) == rank).astype(F32)
-    line_iota = iota((NLINES, CHUNK), 0)
-    cell_iota = iota((G, CHUNK), 0)
-
-    def spread(chunk, total):
-        where = pl.ds(pl.multiple_of(chunk * CHUNK, CHUNK), CHUNK)
-        charge = jnp.concatenate(
-            [
-                halo_ref[4, pl.ds(3 * TILES + chunk * (CHUNK // TILE) + q, 1), :]
-                for q in range(CHUNK // TILE)
-            ],
-            axis=1,
-        )
-        for corner in range(8):
-            cell = cells[corner : corner + 1, where]
-            high, low = split(weights[corner : corner + 1, where] * charge)
-            hit = line_iota == cell // G
-            lines = jnp.concatenate(
-                [
-                    jnp.where(hit, high.astype(F32), 0.0).astype(BF16),
-                    jnp.where(hit, low.astype(F32), 0.0).astype(BF16),
-                ],
-                axis=0,
-            )
-            spots = (cell_iota == cell % G).astype(F32).astype(BF16)
-            total = total + dot_nt(lines, spots)
-        return total
-
-    total = lax.fori_loop(0, TILES * TILE // CHUNK, spread, jnp.zeros((2 * NLINES, G), F32))
-    lines_high, lines_low = split(total[:NLINES] + total[NLINES:])
-    send_ref[:, :CAP, :] = (dot(pick, lines_high) + dot(pick, lines_low)).reshape(ROWS, CAP, G)
+    one, zero = jnp.ones((), BF16), jnp.zeros((), BF16)
+    line_iota = iota((NLINES, atoms), 0).astype(F32).astype(BF16)
+    cell_iota = iota((G, atoms), 0).astype(F32).astype(BF16)
+    charge = jnp.concatenate(
+        [halo_ref[4, 3 * TILES + t : 3 * TILES + t + 1, :] for t in range(TILES)], axis=1
+    )
+
+    def lines_of(corner):
+        cell = cells[corner : corner + 1, :]
+        line = lax.div(cell, G).astype(F32).astype(BF16)
+        return cell, jnp.where(line_iota == line, one, zero)
+
+    total = jnp.zeros((2 * G, NLINES), F32)
+    for corner in range(8):
+        cell, lines = lines_of(corner)
+        high, low = split(weights[corner : corner + 1, :] * charge)
+        hit = cell_iota == lax.rem(cell, G).astype(F32).astype(BF16)
+        spots = jnp.concatenate([jnp.where(hit, high, zero), jnp.where(hit, low, zero)], axis=0)
+        total = total + dot_nt(spots, lines)
+    lines_high, lines_low = split(total[:G] + total[G:])
+    send_ref[:, :CAP, :] = (dot_nt(pick, lines_high) + dot_nt(pick, lines_low)).reshape(
+        ROWS, CAP, G
+    )
     send_ref[:, CAP, :] = dot_nt(owner.astype(BF16), place.astype(BF16))
 
     pl.semaphore_wait(barrier, 2 * (ROWS - 1) + 3 + 4)
 
-    def send_lines(k, carry):
-        row = peer(k)
+    def send_lines(far_group, far_dom):
         remote(
-            send_ref.at[row, pl.ds(0, CAP + 1)], line_buf.at[me, pl.ds(0, CAP + 1)],
-            line_sems.at[0], line_sems.at[1], row, pen,
+            send_ref.at[far_group * 16 + far_dom, pl.ds(0, CAP + 1)],
+            line_buf.at[me, pl.ds(0, CAP + 1)],
+            line_sems.at[0], line_sems.at[1], (far_group, far_dom, pen),
         ).start()
-        return carry
-
-    lax.fori_loop(0, ROWS - 1, send_lines, 0)
+
+    each_peer(send_lines)
     line_buf[me, 0 : CAP + 1, :] = send_ref[me, 0 : CAP + 1, :]
 
     slabs = ((rho_hbm, rho), (sus_hbm, sus), (ion_hbm, ion))
@@ -273,7 +286,7 @@
         return remote(
             source, whole.at[:, columns, :],
             pen_sems.at[0, index, k - 1], pen_sems.at[1, index, k - 1],
-            me, lax.rem(pen + k, PEN),
+            (group, dom, lax.rem(pen + k, PEN)),
         )
 
     for k in (1, 2, 3):
@@ -283,10 +296,11 @@
 
     def halo_copy(dx, dy):
         number = (1 - dx) * 3 + 1 - dy
+        row = lax.rem(me + dx + ROWS, ROWS)
         return remote(
             halo_ref.at[4], halo_ref.at[number], halo_send_sems.at[number],
             halo_recv_sems.at[number],
-            lax.rem(me + dx + ROWS, ROWS), lax.rem(pen + dy + PEN, PEN),
+            (row // 16, lax.rem(row, 16), lax.rem(pen + dy + PEN, PEN)),
         )
 
     for dx, dy in neighbours:
@@ -307,14 +321,14 @@
             BOX_HEIGHT if axis == 2 else 1.0
         )
 
-    def whole_line_copy(ref, sems):
-        most = ref.at[pl.ds(0, ROWS - 1), pl.ds(0, CAP + 1)]
-        return pltpu.make_async_remote_copy(
-            src_ref=most, dst_ref=most, send_sem=sems.at[0], recv_sem=sems.at[1],
-            device_id=device(lax.rem(me + 1, ROWS), pen), device_id_type=MESH,
-        )
-
-    whole_line_copy(line_buf, line_sems).wait_recv()
+    def all_of(ref, send_sem, recv_sem):
+        return remote(ref, ref, send_sem, recv_sem, (group, dom, sibling))
+
+    def all_lines():
+        most = line_buf.at[pl.ds(0, ROWS - 1), pl.ds(0, CAP + 1)]
+        return all_of(most, line_sems.at[0], line_sems.at[1])
+
+    all_lines().wait_recv()
     spread_targets = dot(source_of, line_buf[:, CAP, :].astype(BF16))
     target = jnp.sum(jnp.where(own_lane, spread_targets, 0.0), axis=1, keepdims=True)
     landing = (target == iota((ROWS * CAP, ROWS), 1).astype(F32)).astype(F32)
@@ -328,16 +342,11 @@
     def mm_copy(k):
         return remote(
             mm.at[:, columns, :], mm.at[:, columns, :], mm_sems.at[0, k - 1], mm_sems.at[1, k - 1],
-            me, lax.rem(pen + k, PEN),
+            (group, dom, lax.rem(pen + k, PEN)),
         )
 
     for k in (1, 2, 3):
         mm_copy(k).start()
-    for k in (1, 2, 3):
-        slab_copy(0, k).wait_recv()
-    for k in (1, 2, 3):
-        mm_copy(k).wait_recv()
-
     tile_lane = iota((TILE, TILES), 1)
 
     def own_tile(t, carry):
@@ -365,91 +374,120 @@
         )
         return carry
 
+    for dx, dy in neighbours:
+        halo_copy(dx, dy).wait()
+    for dx, dy in neighbours:
+        outside = (me + dx < 0) | (me + dx >= ROWS) | (pen + dy < 0) | (pen + dy >= PEN)
+
+        @pl.when(outside)
+        def _():
+            halo_ref[(dx + 1) * 3 + dy + 1] = jnp.zeros((4 * TILES, TILE), F32)
+
+    lax.fori_loop(0, AGREE_TILES, own_tile, 0)
+    done = AGREE_TILES
+    for k in (1, 2, 3):
+        slab_copy(0, k).wait_recv()
+    for k in (1, 2, 3):
+        mm_copy(k).wait_recv()
+
+    def square(index):
+        return jnp.concatenate([square_ref[2 * index], square_ref[2 * index + 1]], axis=0)
+
     def wide(index):
         return jnp.concatenate([big_ref[2 * index], big_ref[2 * index + 1]], axis=1)
 
-    done = 0
     low_lanes = iota((ROWS, G), 1) < ROWS
 
+    y_rows = [pl.ds(pl.multiple_of((2 * z + core) * 32, 32), 32) for z in range(2)]
+    y_table = jnp.concatenate([square_ref[part, rows, :] for part in range(2) for rows in y_rows])
+    across, beside = lax.rem(group + 2, 4), lax.rem(group + 3 - 2 * z_lo, 4)
+
+    def fwd_copy(far_group, far_dom, z):
+        return remote(
+            fwd_send.at[z, pl.ds(far_group * 16 + far_dom, 1)], fwd_recv.at[pl.ds(me, 1)],
+            fwd_sems.at[0], fwd_sems.at[1], (far_group, far_dom, 2 * z + core),
+        )
+
     def fwd_all():
-        most_send, most_recv = fwd_send.at[pl.ds(0, ROWS - 1)], fwd_recv.at[pl.ds(0, ROWS - 1)]
-        return pltpu.make_async_remote_copy(
-            src_ref=most_send, dst_ref=most_recv, send_sem=fwd_sems.at[0], recv_sem=fwd_sems.at[1],
-            device_id=device(lax.rem(me + 1, ROWS), pen), device_id_type=MESH,
-        )
-
-    def ret_copy(slot, row, column):
-        return remote(
-            ret_send.at[pl.ds(row, 1)],
+        return all_of(fwd_recv.at[pl.ds(0, ROWS - 1)], fwd_sems.at[0], fwd_sems.at[1])
+
+    def ret_copy(slot, far_group, far_dom, column):
+        return remote(
+            ret_send.at[pl.ds(far_group * 16 + far_dom, 1)],
             ret_recv.at[slot, half, core, z_lo, pl.ds(lax.rem(me, 32), 1)],
-            ret_sems.at[0], ret_sems.at[1 + slot], row, column,
+            ret_sems.at[0], ret_sems.at[1 + slot], (far_group, far_dom, column),
         )
 
     def ret_all(slot):
-        most = ret_send.at[pl.ds(0, 2 * ROWS - 1)]
-        return pltpu.make_async_remote_copy(
-            src_ref=most, dst_ref=most, send_sem=ret_sems.at[0], recv_sem=ret_sems.at[1 + slot],
-            device_id=device(lax.rem(me + 1, ROWS), pen), device_id_type=MESH,
-        )
+        return all_of(ret_send.at[pl.ds(0, 2 * ROWS - 1)], ret_sems.at[0], ret_sems.at[1 + slot])
 
     def core_copy(slot, h):
         return remote(
             ret_recv.at[slot, h, core], ret_recv.at[slot, h, core],
-            core_sems.at[0, slot, h], core_sems.at[1, slot, h], me, sibling,
+            core_sems.at[0, slot, h], core_sems.at[1, slot, h], (group, dom, sibling),
+        )
+
+    def back_copy(far_group, far_dom):
+        return remote(
+            line_send.at[far_group * 16 + far_dom], back_ref.at[me],
+            back_sems.at[0], back_sems.at[1], (far_group, far_dom, pen),
+        )
+
+    def moment_copy(far_group, far_dom):
+        return remote(
+            moment_send, moment_recv.at[pl.ds(me, 1)],
+            moment_sems.at[0], moment_sems.at[1], (far_group, far_dom, pen),
         )
 
     for iteration in range(ITERS):
         slot = iteration % 2
         source = jnp.concatenate([rho[0] + mm[0], rho[1] + mm[1]], axis=1)
-        spectrum = left_const(square_ref[0, columns, :], square_ref[1, columns, :], source)
-        spectrum = right_const(spectrum, wide(0), wide(1))
+        spectrum = right_const(left_const(y_table, source), wide(0), wide(1))
         if iteration > 0:
             fwd_all().wait_send()
-        fwd_send[0:32, :] = spectrum[:, :G]
-        fwd_send[32:64, :] = spectrum[:, G:]
-
-        def send_fwd(k, carry):
-            row = peer(k)
-            remote(
-                fwd_send.at[pl.ds(row, 1)], fwd_recv.at[pl.ds(me, 1)],
-                fwd_sems.at[0], fwd_sems.at[1], row, pen,
-            ).start()
-            return carry
-
-        lax.fori_loop(0, ROWS - 1, send_fwd, 0)
-        fwd_recv[pl.ds(me, 1), :] = fwd_send[pl.ds(me, 1), :]
+        for z in range(2):
+            for h in range(2):
+                fwd_send[z, h * 32 : (h + 1) * 32, :] = spectrum[
+                    z * 32 : (z + 1) * 32, h * G : (h + 1) * G
+                ]
+
+        def send_across(far_dom):
+            fwd_copy(across, far_dom, 1 - z_lo).start()
+
+        def send_beside(far_dom):
+            fwd_copy(beside, far_dom, 1 - z_lo).start()
+            fwd_copy(beside, far_dom, z_lo).start()
+
+        def send_near(far_dom):
+            fwd_copy(group, far_dom, z_lo).start()
+
+        each_x(4, send_across)
+        each_x(4, send_beside)
+        each_x(3, send_near)
+        for y in ys[:3]:
+            send_near(dom_x * 4 + y)
+        fwd_recv[pl.ds(me, 1), :] = fwd_send[z_lo, pl.ds(me, 1), :]
         if iteration == 0:
             for index in (1, 2):
                 for k in (1, 2, 3):
                     slab_copy(index, k).start()
-            for dx, dy in neighbours:
-                halo_copy(dx, dy).wait()
-            for dx, dy in neighbours:
-                outside = (me + dx < 0) | (me + dx >= ROWS) | (pen + dy < 0) | (pen + dy >= PEN)
-
-                @pl.when(outside)
-                def _():
-                    halo_ref[(dx + 1) * 3 + dy + 1] = jnp.zeros((4 * TILES, TILE), F32)
-
         lax.fori_loop(done, done + FWD_TILES, own_tile, 0)
         done += FWD_TILES
         fwd_all().wait_recv()
         received = fwd_recv[...]
         both = jnp.concatenate([received, pltpu.roll(received, ROWS, 1)], axis=0)
-        modes = left_const(square_ref[4], square_ref[5], both) * green[...]
-        solved = left_const(square_ref[6], square_ref[7], modes)
+        modes = left_const(square(2), both) * green[...]
+        solved = left_const(square(3), modes)
         if iteration > 0:
             ret_all(1 - slot).wait_send()
         ret_send[:ROWS, :] = jnp.where(low_lanes, solved[:ROWS], pltpu.roll(solved[ROWS:], ROWS, 1))
 
-        def send_ret(k, carry):
-            row = peer(k)
-            ret_copy(slot, row, other_chip).start()
-            ret_copy(slot, row, pen).start()
-            return carry
-
-        lax.fori_loop(0, ROWS - 1, send_ret, 0)
-        ret_copy(slot, me, other_chip).start()
+        def send_ret(far_group, far_dom):
+            ret_copy(slot, far_group, far_dom, other_chip).start()
+            ret_copy(slot, far_group, far_dom, pen).start()
+
+        each_peer(send_ret)
+        ret_copy(slot, group, dom, other_chip).start()
         ret_recv[slot, half, core, z_lo, pl.ds(lax.rem(me, 32), 1)] = ret_send[pl.ds(me, 1), :]
         lax.fori_loop(done, done + RET_TILES, own_tile, 0)
         done += RET_TILES
@@ -464,11 +502,17 @@
             core_copy(slot, h).wait_recv()
         lines = jnp.concatenate([ret_recv[slot, h].reshape(G, G) for h in range(2)], axis=1)
         lines = right_const(lines, wide(2), wide(3))
-        potential = left_const(square_ref[2], square_ref[3], lines)
+        if iteration == ITERS - 1:
+            own_table = jnp.concatenate([square_ref[part, columns, :] for part in (2, 3)])
+            own_pot = left_const(own_table, lines)
+            own_pot = jnp.concatenate([own_pot[:, x * G : (x + 1) * G] for x in range(2)], axis=0)
+            pot_high, pot_low = split(own_pot)
+            line_send[...] = (dot(landing, pot_high) + dot(landing, pot_low)).reshape(ROWS, CAP, G)
+            each_peer(lambda far_group, far_dom: back_copy(far_group, far_dom).start())
+            back_ref[me] = line_send[me]
+        potential = left_const(square(1), lines)
         for x in range(2):
             own = potential[:, x * G : (x + 1) * G]
-            if iteration == ITERS - 1:
-                last_pot[x] = own
             rho[x] = rho[x] - MIX_RATE * (rho[x] + sus[x] * (own + ion[x]))
         for h in range(2):
             core_copy(slot, h).wait_send()
@@ -483,63 +527,44 @@
     for index, term in enumerate(sums):
         value = jnp.sum(jnp.sum(term, axis=0, keepdims=True), axis=1, keepdims=True)
         own_moments = jnp.where(iota((1, G), 1) == index, value, own_moments)
-    own_pot = jnp.concatenate([last_pot[x, columns, :] for x in range(2)], axis=0)
-    pot_high, pot_low = split(own_pot)
-    line_send[:, :CAP, :] = (dot(landing, pot_high) + dot(landing, pot_low)).reshape(ROWS, CAP, G)
-    line_send[:, CAP, :] = jnp.broadcast_to(own_moments, (ROWS, G))
-
-    def send_back(k, carry):
-        row = peer(k)
-        remote(
-            line_send.at[row, pl.ds(0, CAP + 1)], back_ref.at[me, pl.ds(0, CAP + 1)],
-            back_sems.at[0], back_sems.at[1], row, pen,
-        ).start()
-        return carry
-
-    lax.fori_loop(0, ROWS - 1, send_back, 0)
-    back_ref[me, 0 : CAP + 1, :] = line_send[me, 0 : CAP + 1, :]
+    moment_send[...] = own_moments
+    each_peer(lambda far_group, far_dom: moment_copy(far_group, far_dom).start())
+    moment_recv[pl.ds(me, 1), :] = own_moments
     for x in range(2):
-        pot_out[x] = last_pot[x, columns, :]
+        pot_out[x] = own_pot[x * 32 : (x + 1) * 32]
         rho_out[x] = rho[x, columns, :]
     lax.fori_loop(done, TILES, own_tile, 0)
 
-    whole_line_copy(line_buf, line_sems).wait_send()
+    all_lines().wait_send()
     for k in (1, 2, 3):
         for index in range(3):
             slab_copy(index, k).wait_send()
         mm_copy(k).wait_send()
     fwd_all().wait_send()
     ret_all((ITERS - 1) % 2).wait_send()
-    whole_line_copy(line_send, back_sems).wait()
-
-    back_high, back_low = split(back_ref[:, :CAP, :].reshape(ROWS * CAP, G))
-    values = dot_tn(jnp.concatenate([back_high, back_low], axis=1), pick)
-    values_high, values_low = split(values[:G] + values[G:])
+    all_of(moment_recv.at[pl.ds(0, ROWS - 1)], moment_sems.at[0], moment_sems.at[1]).wait()
+    all_of(back_ref.at[pl.ds(0, ROWS - 1)], back_sems.at[0], back_sems.at[1]).wait()
+
+    back_high, back_low = split(back_ref[...].reshape(ROWS * CAP, G))
+    values_high, values_low = split((dot(pick_t, back_high) + dot(pick_t, back_low)).T)
     values = jnp.concatenate([values_high, values_low], axis=0)
-    moments = jnp.sum(back_ref[:, CAP, :], axis=0, keepdims=True) * (1.0 / (G * math.sqrt(G)))
+    moments = jnp.sum(moment_recv[...], axis=0, keepdims=True) * (1.0 / (G * math.sqrt(G)))
     moment = [
         jnp.sum(jnp.where(iota((1, G), 1) == m, moments, 0.0), axis=1, keepdims=True)
         for m in range(4)
     ]
 
-    def gather(chunk, carry):
-        where = pl.ds(pl.multiple_of(chunk * CHUNK, CHUNK), CHUNK)
-        total = short[:, where]
-        for corner in range(8):
-            cell = cells[corner : corner + 1, where]
-            lines = (line_iota == cell // G).astype(F32).astype(BF16)
-            found = dot(values, lines)
-            found = jnp.where(cell_iota == cell % G, found[:G] + found[G:], 0.0)
-            total = total + weights[corner : corner + 1, where] * jnp.sum(
-                found, axis=0, keepdims=True
-            )
-        for m in range(4):
-            total = total + moment[m] * basis_ref[m : m + 1, where]
-        atom = chunk * CHUNK + iota((1, CHUNK), 1)
-        mm_out[:, where] = jnp.where(atom // TILE < live, total, 0.0)
-        return carry
-
-    lax.fori_loop(0, TILES * TILE // CHUNK, gather, 0)
+    spot_iota = iota((G, atoms), 0)
+    found = jnp.zeros((G, atoms), F32)
+    for corner in range(8):
+        cell, lines = lines_of(corner)
+        weight = jnp.where(spot_iota == lax.rem(cell, G), weights[corner : corner + 1, :], 0.0)
+        halves_found = dot(values, lines)
+        found = found + weight * (halves_found[:G] + halves_found[G:])
+    total = short[...] + jnp.sum(found, axis=0, keepdims=True)
+    for m in range(4):
+        total = total + moment[m] * basis_ref[m : m + 1, :]
+    mm_out[...] = jnp.where(lax.div(iota((1, atoms), 1), TILE) < live, total, 0.0)
 
 
 def shards(
@@ -580,14 +605,15 @@
             buffer((2, G, G), F32),
             buffer((2, G, G), F32),
             buffer((2, G, G), F32),
-            buffer((ROWS, G), F32),
+            buffer((2, ROWS, G), F32),
             buffer((ROWS, G), F32),
             buffer((2 * ROWS, G), F32),
             buffer((2, 2, 2, 2, 32, G), F32),
             buffer((G, G), F32),
-            buffer((ROWS, 16, G), F32),
-            buffer((2, G, G), F32),
-            buffer((ROWS, 16, G), F32),
+            buffer((ROWS, CAP, G), F32),
+            buffer((1, G), F32),
+            buffer((ROWS, G), F32),
+            buffer((ROWS, CAP, G), F32),
             buffer((3, TILE, TILES), F32),
             buffer((1, atoms), F32),
             dma((13,)),
@@ -599,6 +625,7 @@
             dma((2,)),
             dma((3,)),
             dma((2, 2, 2)),
+            dma((2,)),
             dma((2,)),
         ],
         compiler_params=pltpu.CompilerParams(

time: 128 us -> 116 us (0.906)
  Pallas kernels: 124 us -> 112 us
    pallas_call x1, Pallas kernels: 124 us -> 112 us  [shards(): pl.pallas_call(kernel, out_shape=(jax.ShapeDtypeStruct(block, F32), jax.S...]
where the time goes in v3:
time: 116 us
  Pallas kernels  112 us (97%)
  local copies, waits for them, and re-layouts  2.69 us (2%)
  between operations  1.3 us (1%)
    pallas_call x1, Pallas kernels, shards(): pl.pallas_call(kernel, out_shape=(jax.ShapeDtypeStruct(block, F32), jax.S...  112 us
    unnamed x7, local copies, waits for them, and re-layouts  2.69 us

profile of v3, /device:TPU:1, one launch (start us, length us, event | category | flops | bytes accessed | tf_op | source)
XLA Modules:
  0.0 116.0 jit_solution(5011370124140108525)
XLA Ops:
  1.3 112.0 %embed.1 = (f32[2,32,128]{2,1,0:T(8,128)}, f32[2,32,128]{2,1,0:T(8,128)}, f32[1,2048]{1,0:T(1,128)}) custom-call(s32[1,1]{1,0:T(1,128)S(6)} %copy.21.live_ref, s32[16,16]{1,0:T(8,128)} %bitcast.13, s32[8,2048]{1,0:T(8,128)} %bitcast.9, f32[8,2048]{1,0:T(8,128)} %bitcast.10, f32[48,128]{1,0:T(8,128)} %bitcast.12, f32[16,128]{1,0:T(8,128)} %bitcast.14, ...), custom_call_target="tpu_custom_call" | custom-call | tf_op jit(solution)/shard_map/embed/pallas_call | solution.py:582
  113.3 0.0 copy-start
  113.3 1.4 %copy.22 = f32[2,32,128]{2,1,0:T(8,128)} copy(f32[2,32,128]{2,1,0:T(8,128)} %get-tuple-element.12) | data formatting | bytes 65536
  114.7 0.0 copy-done
  114.7 0.0 copy-start.1
  114.7 0.6 copy.23
  115.3 0.1 copy-done.1
  115.4 0.6 copy.24
Async XLA Ops:
  113.3 1.4 %copy-start = (f32[2,32,128]{2,1,0:T(8,128)S(1)}, f32[2,32,128]{2,1,0:T(8,128)}, u32[]{:S(2)}) copy-start(f32[2,32,128]{2,1,0:T(8,128)} %get-tuple-element.13) | copy-start | bytes 98308
  114.7 0.7 copy-start.1

commit v4 on v3

--- a/solution.py
+++ b/solution.py
@@ -103,9 +103,8 @@
     return lax.broadcasted_iota(jnp.int32, shape, dim)
 
 
-AGREE_TILES = 1
-FWD_TILES = 2
-RET_TILES = 1
+FWD_TILES = (2, 2, 2, 2)
+RET_TILES = (2, 2, 2, 1)
 
 
 def pair_values(own, partner):
@@ -122,14 +121,15 @@
 
 
 def kernel(
-    live_ref, nbr_ref, cell_hbm, weight_hbm, positions_hbm, charge_hbm, slab_hbm, target_hbm,
+    live_ref, nbr_hbm, cell_hbm, weight_hbm, positions_hbm, charge_hbm, slab_hbm, target_hbm,
     rho_hbm, sus_hbm, ion_hbm, basis_hbm, square_hbm, big_hbm, flat_hbm,
     pot_out, rho_out, mm_out,
     cells, weights, charges, slab_buf, target_buf, basis_ref, square_ref, big_ref, flat_ref,
     send_ref, line_buf, halo_ref, mm, rho, sus, ion, fwd_send, fwd_recv, ret_send, ret_recv,
     green, line_send, moment_send, moment_recv, back_ref, columns_of, short,
     load_sems, line_sems, pen_sems, mm_sems, halo_send_sems, halo_recv_sems, fwd_sems, ret_sems,
-    core_sems, back_sems, moment_sems,
+    core_sems, back_sems, moment_sems, line_table, weight_table, pot_buf, out_sems,
+    nbr_ref,
 ):
     group, dom, pen = lax.axis_index("group"), lax.axis_index("dom"), lax.axis_index("pen")
     me = group * 16 + dom
@@ -137,7 +137,6 @@
     other_chip = lax.rem(pen + 2, PEN)
     sibling = z_lo * 2 + (1 - core)
     columns = pl.ds(pl.multiple_of(pen * 32, 32), 32)
-    live = live_ref[0, 0]
     atoms = TILES * TILE
 
     first = [
@@ -164,6 +163,7 @@
                 (square_hbm, square_ref),
                 (big_hbm, big_ref),
                 (basis_hbm, basis_ref),
+                (nbr_hbm, nbr_ref),
             )
         )
     ]
@@ -180,28 +180,21 @@
         return lax.rem(2 + 3 * q + (q // 2) * (2 * q - 1), 4)
 
     dom_x, dom_y = dom // 4, lax.rem(dom, 4)
-    ys = [lax.rem(dom_y + offset, 4) for offset in (2, 1, 3, 0)]
-
-    def each_x(count, act):
-        def step(q, carry):
-            far_x = lax.rem(dom_x + ring(q), 4) * 4
-            for y in ys:
-                act(far_x + y)
-            return carry
-
-        lax.fori_loop(0, count, step, 0)
+    offsets = (2, 1, 3, 0)
+    doms = [
+        lax.rem(dom_x + x, 4) * 4 + lax.rem(dom_y + y, 4) for x in offsets for y in offsets
+    ]
 
     def each_peer(act):
         def step(q, carry):
-            far_group = lax.rem(group + ring(q // 4), 4)
-            far_x = lax.rem(dom_x + ring(lax.rem(q, 4)), 4) * 4
-            for y in ys:
-                act(far_group, far_x + y)
+            far_group = lax.rem(group + ring(q), 4)
+            for far_dom in doms:
+                act(far_group, far_dom)
             return carry
 
-        lax.fori_loop(0, 15, step, 0)
-        for y in ys[:3]:
-            act(group, dom_x * 4 + y)
+        lax.fori_loop(0, 3, step, 0)
+        for far_dom in doms[:15]:
+            act(group, far_dom)
 
     barrier = pltpu.get_barrier_semaphore()
 
@@ -225,6 +218,7 @@
 
     for copy in first:
         copy.wait()
+    live = live_ref[0, 0]
     halo_ref[4, 3 * TILES :, :] = jnp.where(iota((TILES, TILE), 0) < live, charges[...], 0.0)
     slab_row = slab_buf[...]
     slab_rows = slab_row.astype(F32)
@@ -239,7 +233,7 @@
     same = (slab_cols == slab_rows) & (iota((NLINES, NLINES), 0) < iota((NLINES, NLINES), 1))
     rank = jnp.sum(same.astype(F32), axis=0, keepdims=True).astype(jnp.int32)
     pick = (iota((ROWS * CAP, NLINES), 0) == slab_row * CAP + rank).astype(F32)
-    pick, pick_t = pick.astype(BF16), pick.T.astype(BF16)
+    pick_high = pick.astype(BF16)
     owner = jnp.where(iota((ROWS, NLINES), 0) == slab_row, target_buf[...].astype(F32), 0.0)
     place = (iota((TILE, NLINES), 0) == rank).astype(F32)
     one, zero = jnp.ones((), BF16), jnp.zeros((), BF16)
@@ -257,12 +251,13 @@
     total = jnp.zeros((2 * G, NLINES), F32)
     for corner in range(8):
         cell, lines = lines_of(corner)
+        line_table[corner] = lines
         high, low = split(weights[corner : corner + 1, :] * charge)
         hit = cell_iota == lax.rem(cell, G).astype(F32).astype(BF16)
         spots = jnp.concatenate([jnp.where(hit, high, zero), jnp.where(hit, low, zero)], axis=0)
         total = total + dot_nt(spots, lines)
     lines_high, lines_low = split(total[:G] + total[G:])
-    send_ref[:, :CAP, :] = (dot_nt(pick, lines_high) + dot_nt(pick, lines_low)).reshape(
+    send_ref[:, :CAP, :] = (dot_nt(pick_high, lines_high) + dot_nt(pick_high, lines_low)).reshape(
         ROWS, CAP, G
     )
     send_ref[:, CAP, :] = dot_nt(owner.astype(BF16), place.astype(BF16))
@@ -313,6 +308,8 @@
     lam_yz = flat_ref[pl.ds(y_row, 1), :] + flat_ref[pl.ds(G + half, 1), :]
     green[...] = 1.0 / (SCREENING + (flat_ref[0:G, :] + lam_yz))
 
+    pick_t = pick.T.astype(BF16)
+
     source_of = iota((ROWS * CAP, ROWS), 0) // CAP == iota((ROWS * CAP, ROWS), 1)
     source_of = source_of.astype(F32).astype(BF16)
     own_lane = iota((ROWS * CAP, G), 1) == lax.rem(iota((ROWS * CAP, G), 0), CAP)
@@ -329,12 +326,14 @@
         return all_of(most, line_sems.at[0], line_sems.at[1])
 
     all_lines().wait_recv()
-    spread_targets = dot(source_of, line_buf[:, CAP, :].astype(BF16))
-    target = jnp.sum(jnp.where(own_lane, spread_targets, 0.0), axis=1, keepdims=True)
-    landing = (target == iota((ROWS * CAP, ROWS), 1).astype(F32)).astype(F32)
-    landing_t = landing.T.astype(BF16)
-    landing = landing.astype(BF16)
-    lines_high, lines_low = split(line_buf[:, :CAP, :].reshape(ROWS * CAP, G))
+    targets = line_buf[:, CAP, :]
+    targets_t = jnp.concatenate([targets, targets], axis=0).T
+    line_of_row = iota((ROWS, ROWS), 0).astype(F32)
+    landing_t = jnp.concatenate(
+        [(targets_t[k : k + 1, :ROWS] == line_of_row).astype(F32) for k in range(CAP)], axis=1
+    ).astype(BF16)
+    received = jnp.concatenate([line_buf[:, k, :] for k in range(CAP)], axis=0)
+    lines_high, lines_low = split(received)
     own_mm = dot(landing_t, lines_high) + dot(landing_t, lines_low)
     for x in range(2):
         mm[x, columns, :] = own_mm[x * 32 : (x + 1) * 32]
@@ -347,6 +346,9 @@
 
     for k in (1, 2, 3):
         mm_copy(k).start()
+    spread_targets = dot(source_of, targets.astype(BF16))
+    target = jnp.sum(jnp.where(own_lane, spread_targets, 0.0), axis=1, keepdims=True)
+    landing = (target == iota((ROWS * CAP, ROWS), 1).astype(F32)).astype(F32).astype(BF16)
     tile_lane = iota((TILE, TILES), 1)
 
     def own_tile(t, carry):
@@ -383,8 +385,7 @@
         def _():
             halo_ref[(dx + 1) * 3 + dy + 1] = jnp.zeros((4 * TILES, TILE), F32)
 
-    lax.fori_loop(0, AGREE_TILES, own_tile, 0)
-    done = AGREE_TILES
+    done = 0
     for k in (1, 2, 3):
         slab_copy(0, k).wait_recv()
     for k in (1, 2, 3):
@@ -461,18 +462,19 @@
         def send_near(far_dom):
             fwd_copy(group, far_dom, z_lo).start()
 
-        each_x(4, send_across)
-        each_x(4, send_beside)
-        each_x(3, send_near)
-        for y in ys[:3]:
-            send_near(dom_x * 4 + y)
+        for far_dom in doms:
+            send_across(far_dom)
+        for far_dom in doms:
+            send_beside(far_dom)
+        for far_dom in doms[:15]:
+            send_near(far_dom)
         fwd_recv[pl.ds(me, 1), :] = fwd_send[z_lo, pl.ds(me, 1), :]
         if iteration == 0:
             for index in (1, 2):
                 for k in (1, 2, 3):
                     slab_copy(index, k).start()
-        lax.fori_loop(done, done + FWD_TILES, own_tile, 0)
-        done += FWD_TILES
+        lax.fori_loop(done, done + FWD_TILES[iteration], own_tile, 0)
+        done += FWD_TILES[iteration]
         fwd_all().wait_recv()
         received = fwd_recv[...]
         both = jnp.concatenate([received, pltpu.roll(received, ROWS, 1)], axis=0)
@@ -489,8 +491,8 @@
         each_peer(send_ret)
         ret_copy(slot, group, dom, other_chip).start()
         ret_recv[slot, half, core, z_lo, pl.ds(lax.rem(me, 32), 1)] = ret_send[pl.ds(me, 1), :]
-        lax.fori_loop(done, done + RET_TILES, own_tile, 0)
-        done += RET_TILES
+        lax.fori_loop(done, done + RET_TILES[iteration], own_tile, 0)
+        done += RET_TILES[iteration]
         ret_all(slot).wait_recv()
         for h in range(2):
             core_copy(slot, h).start()
@@ -531,9 +533,18 @@
     each_peer(lambda far_group, far_dom: moment_copy(far_group, far_dom).start())
     moment_recv[pl.ds(me, 1), :] = own_moments
     for x in range(2):
-        pot_out[x] = own_pot[x * 32 : (x + 1) * 32]
-        rho_out[x] = rho[x, columns, :]
+        pot_buf[x] = own_pot[x * 32 : (x + 1) * 32]
+    stores = [
+        pltpu.make_async_copy(pot_buf, pot_out, out_sems.at[0]),
+        pltpu.make_async_copy(rho.at[:, columns, :], rho_out, out_sems.at[1]),
+    ]
+    for copy in stores:
+        copy.start()
     lax.fori_loop(done, TILES, own_tile, 0)
+    spot_iota = iota((G, atoms), 0)
+    for corner in range(8):
+        spot = lax.rem(cells[corner : corner + 1, :], G)
+        weight_table[corner] = jnp.where(spot_iota == spot, weights[corner : corner + 1, :], 0.0)
 
     all_lines().wait_send()
     for k in (1, 2, 3):
@@ -554,17 +565,21 @@
         for m in range(4)
     ]
 
-    spot_iota = iota((G, atoms), 0)
     found = jnp.zeros((G, atoms), F32)
     for corner in range(8):
-        cell, lines = lines_of(corner)
-        weight = jnp.where(spot_iota == lax.rem(cell, G), weights[corner : corner + 1, :], 0.0)
-        halves_found = dot(values, lines)
-        found = found + weight * (halves_found[:G] + halves_found[G:])
+        halves_found = dot(values, line_table[corner])
+        found = found + weight_table[corner] * (halves_found[:G] + halves_found[G:])
     total = short[...] + jnp.sum(found, axis=0, keepdims=True)
     for m in range(4):
         total = total + moment[m] * basis_ref[m : m + 1, :]
     mm_out[...] = jnp.where(lax.div(iota((1, atoms), 1), TILE) < live, total, 0.0)
+    for copy in stores:
+        copy.wait()
+
+
+def copy_kernel(*refs):
+    for source, target in zip(refs[:3], refs[3:]):
+        target[...] = source[...]
 
 
 def shards(
@@ -572,7 +587,6 @@
     line_target, neighbour_tiles, live_tiles, initial_density, susceptibility, ion_potential,
 ):
     vmem = pl.BlockSpec(memory_space=pltpu.VMEM)
-    smem = pl.BlockSpec(memory_space=pltpu.SMEM)
     hbm = pl.BlockSpec(memory_space=pltpu.HBM)
     atoms = TILES * TILE
     square, big, flat = (jnp.asarray(table) for table in tables())
@@ -586,8 +600,8 @@
             jax.ShapeDtypeStruct(block, F32),
             jax.ShapeDtypeStruct((1, atoms), F32),
         ),
-        in_specs=[smem] * 2 + [hbm] * 13,
-        out_specs=(vmem,) * 3,
+        in_specs=[pl.BlockSpec(memory_space=pltpu.SMEM)] + [hbm] * 14,
+        out_specs=(hbm, hbm, vmem),
         scratch_shapes=[
             buffer((8, atoms), jnp.int32),
             buffer((8, atoms), F32),
@@ -616,7 +630,7 @@
             buffer((ROWS, CAP, G), F32),
             buffer((3, TILE, TILES), F32),
             buffer((1, atoms), F32),
-            dma((13,)),
+            dma((14,)),
             dma((2,)),
             dma((2, 3, 3)),
             dma((2, 3)),
@@ -627,6 +641,11 @@
             dma((2, 2, 2)),
             dma((2,)),
             dma((2,)),
+            buffer((8, NLINES, atoms), BF16),
+            buffer((8, G, atoms), F32),
+            buffer((2, 32, G), F32),
+            dma((2,)),
+            pltpu.SMEM((TILES, NBR), jnp.int32),
         ],
         compiler_params=pltpu.CompilerParams(
             collective_id=0, has_side_effects=True, vmem_limit_bytes=VMEM_LIMIT
@@ -638,6 +657,14 @@
         line_slab.reshape(1, NLINES), line_target[0], initial_density, susceptibility,
         ion_potential, multipole_basis[0, 0], square, big, flat,
     )
+    results = (potential, density, values)
+    potential, density, values = pl.pallas_call(
+        copy_kernel,
+        out_shape=tuple(jax.ShapeDtypeStruct(r.shape, F32) for r in results),
+        in_specs=[vmem] * 3,
+        out_specs=(vmem,) * 3,
+        name="results",
+    )(*results)
     return potential, density, values[None]
 
 

time: 116 us -> 112 us (0.966)
  local copies, waits for them, and re-layouts: 2.69 us -> 0 us
  Pallas kernels: 112 us -> 110 us
    pallas_call x1, Pallas kernels: 112 us -> 109 us  [shards(): pl.pallas_call(kernel, out_shape=(jax.ShapeDtypeStruct(block, F32), jax.S...]
    unnamed x7 -> x0, local copies, waits for them, and re-layouts: 2.69 us -> none
    pallas_call x0 -> x1, Pallas kernels: none -> 1.41 us  [shards(): pl.pallas_call(copy_kernel, out_shape=tuple((jax.ShapeDtypeStruct(r.shape...]
where the time goes in v4:
time: 112 us
  Pallas kernels  110 us (98%)
  between operations  1.29 us (1%)
    pallas_call x1, Pallas kernels, shards(): pl.pallas_call(kernel, out_shape=(jax.ShapeDtypeStruct(block, F32), jax.S...  109 us

profile of v4, /device:TPU:1, one launch (start us, length us, event | category | flops | bytes accessed | tf_op | source)
XLA Modules:
  0.0 111.8 jit_solution(9982172759403713020)
XLA Ops:
  1.3 109.1 %embed.1 = (f32[2,32,128]{2,1,0:T(8,128)}, f32[2,32,128]{2,1,0:T(8,128)}, f32[1,2048]{1,0:T(1,128)}) custom-call(s32[1,1]{1,0:T(1,128)S(6)} %copy.18.live_ref, s32[16,16]{1,0:T(8,128)} %bitcast.13, s32[8,2048]{1,0:T(8,128)} %bitcast.9, f32[8,2048]{1,0:T(8,128)} %bitcast.10, f32[48,128]{1,0:T(8,128)} %bitcast.12, f32[16,128]{1,0:T(8,128)} %bitcast.14, ...), custom_call_target="tpu_custom_call" | custom-call | tf_op jit(solution)/shard_map/embed/pallas_call | solution.py:596
  110.3 1.4 %results.1 = (f32[2,32,128]{2,1,0:T(8,128)}, f32[2,32,128]{2,1,0:T(8,128)}, f32[1,2048]{1,0:T(1,128)}) custom-call(f32[2,32,128]{2,1,0:T(8,128)} %get-tuple-element.9.refs_0_, f32[2,32,128]{2,1,0:T(8,128)} %get-tuple-element.10.refs_1_, f32[1,2048]{1,0:T(1,128)} %get-tuple-element.11.refs_2_), custom_call_target="tpu_custom_call" | custom-call | tf_op jit(solution)/shard_map/results/pallas_call | solution.py:661

commit v5 on v4

--- a/solution.py
+++ b/solution.py
@@ -103,8 +103,8 @@
     return lax.broadcasted_iota(jnp.int32, shape, dim)
 
 
-FWD_TILES = (2, 2, 2, 2)
-RET_TILES = (2, 2, 2, 1)
+FWD_TILES = (0, 2, 2, 2)
+RET_TILES = (2, 2, 2, 2)
 
 
 def pair_values(own, partner):
@@ -264,6 +264,19 @@
 
     pl.semaphore_wait(barrier, 2 * (ROWS - 1) + 3 + 4)
 
+    slabs = ((rho_hbm, rho), (sus_hbm, sus), (ion_hbm, ion))
+
+    def slab_copy(index, k):
+        source, whole = slabs[index]
+        return remote(
+            source, whole.at[:, columns, :],
+            pen_sems.at[0, index, k - 1], pen_sems.at[1, index, k - 1],
+            (group, dom, lax.rem(pen + k, PEN)),
+        )
+
+    for k in (1, 2, 3):
+        slab_copy(0, k).start()
+
     def send_lines(far_group, far_dom):
         remote(
             send_ref.at[far_group * 16 + far_dom, pl.ds(0, CAP + 1)],
@@ -274,19 +287,6 @@
     each_peer(send_lines)
     line_buf[me, 0 : CAP + 1, :] = send_ref[me, 0 : CAP + 1, :]
 
-    slabs = ((rho_hbm, rho), (sus_hbm, sus), (ion_hbm, ion))
-
-    def slab_copy(index, k):
-        source, whole = slabs[index]
-        return remote(
-            source, whole.at[:, columns, :],
-            pen_sems.at[0, index, k - 1], pen_sems.at[1, index, k - 1],
-            (group, dom, lax.rem(pen + k, PEN)),
-        )
-
-    for k in (1, 2, 3):
-        slab_copy(0, k).start()
-
     neighbours = [(dx, dy) for dx in (-1, 0, 1) for dy in (-1, 0, 1) if (dx, dy) != (0, 0)]
 
     def halo_copy(dx, dy):
@@ -298,8 +298,6 @@
             (row // 16, lax.rem(row, 16), lax.rem(pen + dy + PEN, PEN)),
         )
 
-    for dx, dy in neighbours:
-        halo_copy(dx, dy).start()
     for copy in later:
         copy.wait()
 
@@ -376,15 +374,6 @@
         )
         return carry
 
-    for dx, dy in neighbours:
-        halo_copy(dx, dy).wait()
-    for dx, dy in neighbours:
-        outside = (me + dx < 0) | (me + dx >= ROWS) | (pen + dy < 0) | (pen + dy >= PEN)
-
-        @pl.when(outside)
-        def _():
-            halo_ref[(dx + 1) * 3 + dy + 1] = jnp.zeros((4 * TILES, TILE), F32)
-
     done = 0
     for k in (1, 2, 3):
         slab_copy(0, k).wait_recv()
@@ -470,6 +459,8 @@
             send_near(far_dom)
         fwd_recv[pl.ds(me, 1), :] = fwd_send[z_lo, pl.ds(me, 1), :]
         if iteration == 0:
+            for dx, dy in neighbours:
+                halo_copy(dx, dy).start()
             for index in (1, 2):
                 for k in (1, 2, 3):
                     slab_copy(index, k).start()
@@ -491,6 +482,16 @@
         each_peer(send_ret)
         ret_copy(slot, group, dom, other_chip).start()
         ret_recv[slot, half, core, z_lo, pl.ds(lax.rem(me, 32), 1)] = ret_send[pl.ds(me, 1), :]
+        if iteration == 0:
+            for dx, dy in neighbours:
+                halo_copy(dx, dy).wait()
+            for dx, dy in neighbours:
+                outside = (me + dx < 0) | (me + dx >= ROWS) | (pen + dy < 0) | (pen + dy >= PEN)
+
+                @pl.when(outside)
+                def _():
+                    halo_ref[(dx + 1) * 3 + dy + 1] = jnp.zeros((4 * TILES, TILE), F32)
+
         lax.fori_loop(done, done + RET_TILES[iteration], own_tile, 0)
         done += RET_TILES[iteration]
         ret_all(slot).wait_recv()
@@ -565,11 +566,15 @@
         for m in range(4)
     ]
 
-    found = jnp.zeros((G, atoms), F32)
-    for corner in range(8):
-        halves_found = dot(values, line_table[corner])
-        found = found + weight_table[corner] * (halves_found[:G] + halves_found[G:])
-    total = short[...] + jnp.sum(found, axis=0, keepdims=True)
+    parts = []
+    for start in range(0, atoms, 256):
+        where = slice(start, start + 256)
+        found = jnp.zeros((G, 256), F32)
+        for corner in range(8):
+            both = dot(values, line_table[corner, :, where])
+            found = found + weight_table[corner, :, where] * (both[:G] + both[G:])
+        parts.append(jnp.sum(found, axis=0, keepdims=True))
+    total = short[...] + jnp.concatenate(parts, axis=1)
     for m in range(4):
         total = total + moment[m] * basis_ref[m : m + 1, :]
     mm_out[...] = jnp.where(lax.div(iota((1, atoms), 1), TILE) < live, total, 0.0)

time: 112 us -> 114 us (1.018)
  Pallas kernels: 110 us -> 112 us
    pallas_call x1, Pallas kernels: 109 us -> 111 us  [shards(): pl.pallas_call(kernel, out_shape=(jax.ShapeDtypeStruct(block, F32), jax.S...]
where the time goes in v5:
time: 114 us; the launch traced here: 113 us
  Pallas kernels  112 us (98%)
  between operations  1.29 us (1%)
    pallas_call x1, Pallas kernels, shards(): pl.pallas_call(kernel, out_shape=(jax.ShapeDtypeStruct(block, F32), jax.S...  111 us

profile of v5, /device:TPU:1, one launch (start us, length us, event | category | flops | bytes accessed | tf_op | source)
XLA Modules:
  0.0 113.4 jit_solution(14451560633252961520)
XLA Ops:
  1.3 110.7 %embed.1 = (f32[2,32,128]{2,1,0:T(8,128)}, f32[2,32,128]{2,1,0:T(8,128)}, f32[1,2048]{1,0:T(1,128)}) custom-call(s32[1,1]{1,0:T(1,128)S(6)} %copy.18.live_ref, s32[16,16]{1,0:T(8,128)} %bitcast.13, s32[8,2048]{1,0:T(8,128)} %bitcast.9, f32[8,2048]{1,0:T(8,128)} %bitcast.10, f32[48,128]{1,0:T(8,128)} %bitcast.12, f32[16,128]{1,0:T(8,128)} %bitcast.14, ...), custom_call_target="tpu_custom_call" | custom-call | tf_op jit(solution)/shard_map/embed/pallas_call | solution.py:601
  112.0 1.4 %results.1 = (f32[2,32,128]{2,1,0:T(8,128)}, f32[2,32,128]{2,1,0:T(8,128)}, f32[1,2048]{1,0:T(1,128)}) custom-call(f32[2,32,128]{2,1,0:T(8,128)} %get-tuple-element.9.refs_0_, f32[2,32,128]{2,1,0:T(8,128)} %get-tuple-element.10.refs_1_, f32[1,2048]{1,0:T(1,128)} %get-tuple-element.11.refs_2_), custom_call_target="tpu_custom_call" | custom-call | tf_op jit(solution)/shard_map/results/pallas_call | solution.py:666

commit v6 on v4

--- a/solution.py
+++ b/solution.py
@@ -128,7 +128,7 @@
     send_ref, line_buf, halo_ref, mm, rho, sus, ion, fwd_send, fwd_recv, ret_send, ret_recv,
     green, line_send, moment_send, moment_recv, back_ref, columns_of, short,
     load_sems, line_sems, pen_sems, mm_sems, halo_send_sems, halo_recv_sems, fwd_sems, ret_sems,
-    core_sems, back_sems, moment_sems, line_table, weight_table, pot_buf, out_sems,
+    back_sems, moment_sems, line_table, weight_table, pot_buf, out_sems,
     nbr_ref,
 ):
     group, dom, pen = lax.axis_index("group"), lax.axis_index("dom"), lax.axis_index("pen")
@@ -203,16 +203,12 @@
 
     def greet(far_group, far_dom):
         signal(far_group, far_dom, pen)
-        signal(far_group, far_dom, other_chip)
+        for k in (2, 1, 3):
+            signal(far_group, far_dom, lax.rem(pen + k, PEN))
 
     each_peer(greet)
     for k in (1, 2, 3):
         signal(group, dom, lax.rem(pen + k, PEN))
-    for dx in (1, ROWS - 1):
-        for dy in (1, PEN - 1):
-            row = lax.rem(me + dx, ROWS)
-            signal(row // 16, lax.rem(row, 16), lax.rem(pen + dy, PEN))
-
     for copy in later:
         copy.start()
 
@@ -262,7 +258,7 @@
     )
     send_ref[:, CAP, :] = dot_nt(owner.astype(BF16), place.astype(BF16))
 
-    pl.semaphore_wait(barrier, 2 * (ROWS - 1) + 3 + 4)
+    pl.semaphore_wait(barrier, PEN * ROWS - 1)
 
     def send_lines(far_group, far_dom):
         remote(
@@ -420,13 +416,7 @@
         )
 
     def ret_all(slot):
-        return all_of(ret_send.at[pl.ds(0, 2 * ROWS - 1)], ret_sems.at[0], ret_sems.at[1 + slot])
-
-    def core_copy(slot, h):
-        return remote(
-            ret_recv.at[slot, h, core], ret_recv.at[slot, h, core],
-            core_sems.at[0, slot, h], core_sems.at[1, slot, h], (group, dom, sibling),
-        )
+        return all_of(ret_send.at[pl.ds(0, PEN * ROWS - 1)], ret_sems.at[0], ret_sems.at[1 + slot])
 
     def back_copy(far_group, far_dom):
         return remote(
@@ -485,23 +475,20 @@
         ret_send[:ROWS, :] = jnp.where(low_lanes, solved[:ROWS], pltpu.roll(solved[ROWS:], ROWS, 1))
 
         def send_ret(far_group, far_dom):
-            ret_copy(slot, far_group, far_dom, other_chip).start()
-            ret_copy(slot, far_group, far_dom, pen).start()
+            for k in (2, 3, 1, 0):
+                ret_copy(slot, far_group, far_dom, lax.rem(pen + k, PEN)).start()
 
         each_peer(send_ret)
-        ret_copy(slot, group, dom, other_chip).start()
+        for k in (2, 3, 1):
+            ret_copy(slot, group, dom, lax.rem(pen + k, PEN)).start()
         ret_recv[slot, half, core, z_lo, pl.ds(lax.rem(me, 32), 1)] = ret_send[pl.ds(me, 1), :]
         lax.fori_loop(done, done + RET_TILES[iteration], own_tile, 0)
         done += RET_TILES[iteration]
         ret_all(slot).wait_recv()
-        for h in range(2):
-            core_copy(slot, h).start()
         if iteration == 0:
             for index in (1, 2):
                 for k in (1, 2, 3):
                     slab_copy(index, k).wait_recv()
-        for h in range(2):
-            core_copy(slot, h).wait_recv()
         lines = jnp.concatenate([ret_recv[slot, h].reshape(G, G) for h in range(2)], axis=1)
         lines = right_const(lines, wide(2), wide(3))
         if iteration == ITERS - 1:
@@ -516,8 +503,6 @@
         for x in range(2):
             own = potential[:, x * G : (x + 1) * G]
             rho[x] = rho[x] - MIX_RATE * (rho[x] + sus[x] * (own + ion[x]))
-        for h in range(2):
-            core_copy(slot, h).wait_send()
 
     row_u = 1.0 + 2.0 * (iota((G, G), 0).astype(F32) + 0.5) / G
     lane_u = 1.0 + 2.0 * (iota((G, G), 1).astype(F32) + 0.5) / G
@@ -565,11 +550,15 @@
         for m in range(4)
     ]
 
-    found = jnp.zeros((G, atoms), F32)
-    for corner in range(8):
-        halves_found = dot(values, line_table[corner])
-        found = found + weight_table[corner] * (halves_found[:G] + halves_found[G:])
-    total = short[...] + jnp.sum(found, axis=0, keepdims=True)
+    parts = []
+    for start in range(0, atoms, 256):
+        where = slice(start, start + 256)
+        found = jnp.zeros((G, 256), F32)
+        for corner in range(8):
+            both = dot(values, line_table[corner, :, where])
+            found = found + weight_table[corner, :, where] * (both[:G] + both[G:])
+        parts.append(jnp.sum(found, axis=0, keepdims=True))
+    total = short[...] + jnp.concatenate(parts, axis=1)
     for m in range(4):
         total = total + moment[m] * basis_ref[m : m + 1, :]
     mm_out[...] = jnp.where(lax.div(iota((1, atoms), 1), TILE) < live, total, 0.0)
@@ -621,7 +610,7 @@
             buffer((2, G, G), F32),
             buffer((2, ROWS, G), F32),
             buffer((ROWS, G), F32),
-            buffer((2 * ROWS, G), F32),
+            buffer((PEN * ROWS, G), F32),
             buffer((2, 2, 2, 2, 32, G), F32),
             buffer((G, G), F32),
             buffer((ROWS, CAP, G), F32),
@@ -638,7 +627,6 @@
             dma((9,)),
             dma((2,)),
             dma((3,)),
-            dma((2, 2, 2)),
             dma((2,)),
             dma((2,)),
             buffer((8, NLINES, atoms), BF16),

time: 112 us -> 111 us (level)
    pallas_call x1, Pallas kernels: 109 us -> 107 us  [shards(): pl.pallas_call(kernel, out_shape=(jax.ShapeDtypeStruct(block, F32), jax.S...]
where the time goes in v6:
time: 111 us; the launch traced here: 110 us
  Pallas kernels  109 us (98%)
  between operations  1.29 us (1%)
    pallas_call x1, Pallas kernels, shards(): pl.pallas_call(kernel, out_shape=(jax.ShapeDtypeStruct(block, F32), jax.S...  107 us

profile of v6, /device:TPU:1, one launch (start us, length us, event | category | flops | bytes accessed | tf_op | source)
XLA Modules:
  0.0 110.2 jit_solution(7933365668404766126)
XLA Ops:
  1.3 107.5 %embed.1 = (f32[2,32,128]{2,1,0:T(8,128)}, f32[2,32,128]{2,1,0:T(8,128)}, f32[1,2048]{1,0:T(1,128)}) custom-call(s32[1,1]{1,0:T(1,128)S(6)} %copy.18.live_ref, s32[16,16]{1,0:T(8,128)} %bitcast.13, s32[8,2048]{1,0:T(8,128)} %bitcast.9, f32[8,2048]{1,0:T(8,128)} %bitcast.10, f32[48,128]{1,0:T(8,128)} %bitcast.12, f32[16,128]{1,0:T(8,128)} %bitcast.14, ...), custom_call_target="tpu_custom_call" | custom-call | tf_op jit(solution)/shard_map/embed/pallas_call | solution.py:585
  108.8 1.4 %results.1 = (f32[2,32,128]{2,1,0:T(8,128)}, f32[2,32,128]{2,1,0:T(8,128)}, f32[1,2048]{1,0:T(1,128)}) custom-call(f32[2,32,128]{2,1,0:T(8,128)} %get-tuple-element.9.refs_0_, f32[2,32,128]{2,1,0:T(8,128)} %get-tuple-element.10.refs_1_, f32[1,2048]{1,0:T(1,128)} %get-tuple-element.11.refs_2_), custom_call_target="tpu_custom_call" | custom-call | tf_op jit(solution)/shard_map/results/pallas_call | solution.py:649
